TPU v7x, 256 devices: a whole 4x4x8 slice. The times are simulated.
256 devices in a mesh: pole: 16 (over z, x_hi), lat: 4 (over x_lo, core), lon: 4 (over y).
Axes of the slice: x: 4 (x_hi: 2, x_lo: 2; x = x_hi * 2 + x_lo), y: 4, z: 8, core: 2. Of those that a mesh axis runs over, the one named last changes fastest.
Arguments:
- height: float32 [512, 4096], P(('lat', 'pole'), 'lon'), may hold values from -6 to 6
- east_wind: float32 [512, 4096], P(('lat', 'pole'), 'lon'), may hold values from -6 to 6
- north_wind: float32 [512, 4096], P(('lat', 'pole'), 'lon'), may hold values from -6 to 6
- depth: float32 [512, 4096], P('lat', 'lon'), may hold values from 0.5 to 2
- pole_real: float32 [16], P('pole'), may hold values from 0.5 to 2
- pole_imag: float32 [16], P('pole'), may hold values from -1.5 to 1.5
- weight_real: float32 [16], P('pole'), may hold values from -1 to 1
- weight_imag: float32 [16], P('pole'), may hold values from -1 to 1
Outputs:
- new_height: float32 [512, 4096], P(('lat', 'pole'), 'lon')
All inputs are finite; a program needn't handle non-finite values.
Results may differ from a plain program's by a relative error of at most 0.000046.
Values sent between devices are 32-bit elements; how exact they have to be, the bound alone decides.
No kernel may reach another device: no remote copies, remote signals or barrier semaphores. Data moves between devices by JAX's collectives and lax.ppermute only.
A program may use at most 64 MiB of HBM per device.

v0:
```python
import math

import jax
import jax.numpy as jnp
from jax import lax
from jax.sharding import PartitionSpec as P

SWEEPS = 6


coriolis_max = 1.0
zonal_coupling = 1.0
merid_coupling = 1.0
flux_scale = 0.5
north_scale = 0.25
relax_weights = (0.8, 1.0, 0.9, 1.0, 0.85, 1.0)


def padded_2(cells, sides, width):
    for axis, dim in sides:
        count = lax.axis_size(axis)
        head = lax.slice_in_dim(cells, 0, width, axis=dim)
        tail = lax.slice_in_dim(cells, cells.shape[dim] - width, cells.shape[dim], axis=dim)
        cells = jnp.concatenate(
            [
                lax.ppermute(tail, axis, [(i, (i + 1) % count) for i in range(count)]),
                cells,
                lax.ppermute(head, axis, [((i + 1) % count, i) for i in range(count)]),
            ],
            axis=dim,
        )
    return cells


def row_terms(row_index, total_rows):
    theta = math.pi * ((row_index + 0.5) / total_rows - 0.5)
    cosine = jnp.cos(theta)
    coriolis = coriolis_max * jnp.sin(theta)
    coriolis_sq = coriolis * coriolis
    zonal_coef = zonal_coupling / (cosine * cosine + 0.01)
    east_coef = flux_scale / (cosine + 0.05)
    return (coriolis_sq[:, None], zonal_coef[:, None], east_coef[:, None])


def sweep_from(padded, rhs, depth, zonal_coef, diag_real, diag_imag, inv_real, inv_imag, weight):
    centre = padded[:, 1:-1, 1:-1]
    zonal_sum = padded[:, 1:-1, 2:] + padded[:, 1:-1, :-2]
    merid_sum = padded[:, 2:, 1:-1] + padded[:, :-2, 1:-1]
    neigh = depth * (zonal_coef * zonal_sum + merid_coupling * merid_sum)
    phi_real = centre[0]
    phi_imag = centre[1]
    res_real = rhs + neigh[0] - (diag_real * phi_real - diag_imag * phi_imag)
    res_imag = neigh[1] - (diag_real * phi_imag + diag_imag * phi_real)
    new_real = phi_real + weight * (res_real * inv_real - res_imag * inv_imag)
    new_imag = phi_imag + weight * (res_real * inv_imag + res_imag * inv_real)
    return jnp.stack([new_real, new_imag])


def body(height, east_wind, north_wind, depth, pole_real, pole_imag, weight_real, weight_imag):
    block_rows = depth.shape[0]
    total_rows = block_rows * lax.axis_size("lat")
    first_row = lax.axis_index("lat") * block_rows

    def valid_rows(offset, count):
        index_rows = first_row + offset + jnp.arange(count, dtype=jnp.int32)
        inside = jnp.logical_and(index_rows >= 0, index_rows < total_rows)
        return (inside.astype(jnp.float32), index_rows.astype(jnp.float32))

    unused_mask, block_index = valid_rows(0, block_rows)
    coriolis_sq, zonal_coef, east_coef = row_terms(block_index, total_rows)
    edge_mask, unused_index = valid_rows(-1, block_rows + 2)
    height_block, east_block, north_block = (
        lax.all_gather(height, "pole", axis=0, tiled=True),
        lax.all_gather(east_wind, "pole", axis=0, tiled=True),
        lax.all_gather(north_wind, "pole", axis=0, tiled=True),
    )
    winds = padded_2(jnp.stack([east_block, north_block]), (("lat", 1), ("lon", 2)), 1)
    winds = winds * edge_mask[None, :, None]
    partial_value = height_block - east_coef * (winds[0, 1:-1, 2:] - winds[0, 1:-1, :-2])
    rhs = partial_value - north_scale * (winds[1, 2:, 1:-1] - winds[1, :-2, 1:-1])
    real_part = pole_real[0]
    imag_part = pole_imag[0]
    diag_base = coriolis_sq + 2.0 * depth * (zonal_coef + merid_coupling)
    diag_real = real_part + diag_base
    denom = diag_real * diag_real + imag_part * imag_part
    inv_real = diag_real / denom
    inv_imag = -imag_part / denom
    phi = jnp.stack([rhs * inv_real, rhs * inv_imag])
    for step in range(SWEEPS):
        padded = padded_2(phi, (("lat", 1), ("lon", 2)), 1)
        padded = padded * edge_mask[None, :, None]
        phi = sweep_from(
            padded,
            rhs,
            depth,
            zonal_coef,
            diag_real,
            imag_part,
            inv_real,
            inv_imag,
            relax_weights[step],
        )
    weighted = weight_real[0] * phi[0] - weight_imag[0] * phi[1]
    return lax.psum_scatter(weighted, "pole", scatter_dimension=0, tiled=True)


def solution(mesh):
    in_specs = (
        P(("lat", "pole"), "lon"),
        P(("lat", "pole"), "lon"),
        P(("lat", "pole"), "lon"),
        P("lat", "lon"),
        P("pole"),
        P("pole"),
        P("pole"),
        P("pole"),
    )
    out_specs = P(("lat", "pole"), "lon")
    return jax.shard_map(body, mesh=mesh, in_specs=in_specs, out_specs=out_specs, check_vma=False)
```

profile of v0, /device:TPU:8, one launch (start us, length us, event | category | flops | bytes accessed | tf_op | source)
XLA Modules:
  0.0 446.5 jit_solution(15084791205566900717)
XLA Ops:
  6.5 47.2 %all_gather.10 = f32[128,1024]{1,0:T(8,128)S(1)} all-gather(f32[8,1024]{1,0:T(8,128)} %param.9), channel_id=1, replica_groups=mesh['pole'=16,'lat'=4,'lon'=4] {'pole'}, dimensions={0}, use_global_device_ids=true | all-gather | bytes 557056 | tf_op jit(solution)/shard_map/all_gather | solution.py:74
  53.8 38.8 %all_gather.11 = f32[128,1024]{1,0:T(8,128)S(1)} all-gather(f32[8,1024]{1,0:T(8,128)} %param.10), channel_id=1, replica_groups=mesh['pole'=16,'lat'=4,'lon'=4] {'pole'}, dimensions={0}, use_global_device_ids=true | all-gather | bytes 557056 | tf_op jit(solution)/shard_map/all_gather | solution.py:75
  92.7 1.7 collective-permute-start.1
  94.5 42.3 %all_gather.9 = f32[128,1024]{1,0:T(8,128)S(1)} all-gather(f32[8,1024]{1,0:T(8,128)S(1)} %copy-done.16), channel_id=1, replica_groups=mesh['pole'=16,'lat'=4,'lon'=4] {'pole'}, dimensions={0}, use_global_device_ids=true | all-gather | bytes 557056 | tf_op jit(solution)/shard_map/all_gather | solution.py:73
  137.1 1.7 collective-permute-start.2
  140.6 1.7 collective-permute-done.2
  146.7 1.7 collective-permute-start.5
  152.8 3.4 collective-permute-done.6
  157.3 1.7 concatenate.45
  161.7 1.9 collective-permute-start.9
  167.3 4.4 collective-permute-done.10
  172.9 1.7 concatenate.47
  177.3 1.7 collective-permute-start.13
  180.6 1.7 collective-permute-start.14
  182.7 4.4 collective-permute-done.14
  193.2 1.7 collective-permute-start.17
  196.6 1.8 collective-permute-start.18
  198.9 4.2 collective-permute-done.18
  203.1 1.9 collective-permute-done.19
  209.3 1.7 collective-permute-start.21
  214.8 4.3 collective-permute-done.22
  225.1 1.7 collective-permute-start.25
  231.9 3.0 collective-permute-done.26
  241.4 197.8 %reduce-scatter.2.cloned.1.call-done = f32[8,1024]{1,0:T(8,128)} async-done(((f32[128,1024]{1,0:T(8,128)}), f32[8,1024]{1,0:T(8,128)}) %reduce-scatter.2.cloned.1.call-update) | async-done | bytes 32784 | tf_op jit(solution)/shard_map/reduce_scatter | solution.py:104
  (137 shorter events, 55.1 us)
Async XLA Ops:
  6.5 432.7 %reduce-scatter.2.cloned.1.call-start = ((), (), s32[]{:S(2)}) async-start(), calls=%async_computation.1 | async-start | bytes 557056 | tf_op jit(solution)/shard_map/reduce_scatter | solution.py:104
  92.6 44.2 %collective-permute-start = (f32[2,1,1024]{2,1,0:T(1,128)S(1)}, f32[2,1,1024]{2,1,0:T(1,128)S(1)}, u32[]{:S(2)}, u32[]{:S(2)}) collective-permute-start(f32[2,1,1024]{2,1,0:T(1,128)S(1)} %get-tuple-element.43), channel_id=1, source_target_pairs={{0,4},{4,8},{8,12},{12,0},{1,5},{5,9},{9,13},{13,1},{2,6},{6,10},{... | collective-permute-start | bytes 24584 | tf_op jit(solution)/shard_map/ppermute | solution.py:26
  92.7 44.1 %collective-permute-start.1 = (f32[2,1,1024]{2,1,0:T(1,128)S(1)}, f32[2,1,1024]{2,1,0:T(1,128)S(1)}, u32[]{:S(2)}, u32[]{:S(2)}) collective-permute-start(f32[2,1,1024]{2,1,0:T(1,128)S(1)} %get-tuple-element.44), channel_id=1, source_target_pairs={{4,0},{8,4},{12,8},{0,12},{5,1},{9,5},{13,9},{1,13},{6,2},{10,6},{... | collective-permute-start | bytes 24584 | tf_op jit(solution)/shard_map/ppermute | solution.py:28
  137.1 5.1 %collective-permute-start.2 = (f32[2,130,1]{2,1,0:T(8,128)S(1)}, f32[2,130,1]{2,1,0:T(8,128)S(1)}, u32[]{:S(2)}, u32[]{:S(2)}) collective-permute-start(f32[2,130,1]{2,1,0:T(8,128)S(1)} %get-tuple-element.30), channel_id=1, source_target_pairs={{0,1},{1,2},{2,3},{3,0},{4,5},{5,6},{6,7},{7,4},{8,9},{9,10},{10,1... | collective-permute-start | bytes 3128 | tf_op jit(solution)/shard_map/ppermute | solution.py:26
  138.8 5.1 %collective-permute-start.3 = (f32[2,130,1]{2,1,0:T(8,128)S(1)}, f32[2,130,1]{2,1,0:T(8,128)S(1)}, u32[]{:S(2)}, u32[]{:S(2)}) collective-permute-start(f32[2,130,1]{2,1,0:T(8,128)S(1)} %get-tuple-element.29), channel_id=1, source_target_pairs={{1,0},{2,1},{3,2},{0,3},{5,4},{6,5},{7,6},{4,7},{9,8},{10,9},{11,1... | collective-permute-start | bytes 3128 | tf_op jit(solution)/shard_map/ppermute | solution.py:28
  146.6 3.2 collective-permute-start.4
  150.1 6.1 %collective-permute-start.6 = (f32[2,130,1]{2,1,0:T(8,128)S(1)}, f32[2,130,1]{2,1,0:T(8,128)S(1)}, u32[]{:S(2)}, u32[]{:S(2)}) collective-permute-start(f32[2,130,1]{2,1,0:T(8,128)S(1)} %get-tuple-element.28), channel_id=1, source_target_pairs={{0,1},{1,2},{2,3},{3,0},{4,5},{5,6},{6,7},{7,4},{8,9},{9,10},{10,1... | collective-permute-start | bytes 3128 | tf_op jit(solution)/shard_map/ppermute | solution.py:26
  151.4 5.9 %collective-permute-start.7 = (f32[2,130,1]{2,1,0:T(8,128)S(1)}, f32[2,130,1]{2,1,0:T(8,128)}, u32[]{:S(2)}, u32[]{:S(2)}) collective-permute-start(f32[2,130,1]{2,1,0:T(8,128)S(1)} %get-tuple-element.27), channel_id=1, source_target_pairs={{1,0},{2,1},{3,2},{0,3},{5,4},{6,5},{7,6},{4,7},{9,8},{10,9},{11,1... | collective-permute-start | bytes 3128 | tf_op jit(solution)/shard_map/ppermute | solution.py:28
  161.6 3.2 collective-permute-start.8
  161.7 3.2 collective-permute-start.9
  165.2 6.5 %collective-permute-start.10 = (f32[2,130,1]{2,1,0:T(8,128)S(1)}, f32[2,130,1]{2,1,0:T(8,128)S(1)}, u32[]{:S(2)}, u32[]{:S(2)}) collective-permute-start(f32[2,130,1]{2,1,0:T(8,128)S(1)} %get-tuple-element.26), channel_id=1, source_target_pairs={{0,1},{1,2},{2,3},{3,0},{4,5},{5,6},{6,7},{7,4},{8,9},{9,10},{10,1... | collective-permute-start | bytes 3128 | tf_op jit(solution)/shard_map/ppermute | solution.py:26
  166.7 6.2 %collective-permute-start.11 = (f32[2,130,1]{2,1,0:T(8,128)S(1)}, f32[2,130,1]{2,1,0:T(8,128)}, u32[]{:S(2)}, u32[]{:S(2)}) collective-permute-start(f32[2,130,1]{2,1,0:T(8,128)S(1)} %get-tuple-element.25), channel_id=1, source_target_pairs={{1,0},{2,1},{3,2},{0,3},{5,4},{6,5},{7,6},{4,7},{9,8},{10,9},{11,1... | collective-permute-start | bytes 3128 | tf_op jit(solution)/shard_map/ppermute | solution.py:28
  177.2 3.2 collective-permute-start.12
  180.6 6.5 %collective-permute-start.14 = (f32[2,130,1]{2,1,0:T(8,128)S(1)}, f32[2,130,1]{2,1,0:T(8,128)S(1)}, u32[]{:S(2)}, u32[]{:S(2)}) collective-permute-start(f32[2,130,1]{2,1,0:T(8,128)S(1)} %get-tuple-element.24), channel_id=1, source_target_pairs={{0,1},{1,2},{2,3},{3,0},{4,5},{5,6},{6,7},{7,4},{8,9},{9,10},{10,1... | collective-permute-start | bytes 3128 | tf_op jit(solution)/shard_map/ppermute | solution.py:26
  182.3 6.5 %collective-permute-start.15 = (f32[2,130,1]{2,1,0:T(8,128)S(1)}, f32[2,130,1]{2,1,0:T(8,128)}, u32[]{:S(2)}, u32[]{:S(2)}) collective-permute-start(f32[2,130,1]{2,1,0:T(8,128)S(1)} %get-tuple-element.23), channel_id=1, source_target_pairs={{1,0},{2,1},{3,2},{0,3},{5,4},{6,5},{7,6},{4,7},{9,8},{10,9},{11,1... | collective-permute-start | bytes 3128 | tf_op jit(solution)/shard_map/ppermute | solution.py:28
  193.1 3.2 collective-permute-start.16
  196.6 6.5 %collective-permute-start.18 = (f32[2,130,1]{2,1,0:T(8,128)S(1)}, f32[2,130,1]{2,1,0:T(8,128)S(1)}, u32[]{:S(2)}, u32[]{:S(2)}) collective-permute-start(f32[2,130,1]{2,1,0:T(8,128)S(1)} %get-tuple-element.22), channel_id=1, source_target_pairs={{0,1},{1,2},{2,3},{3,0},{4,5},{5,6},{6,7},{7,4},{8,9},{9,10},{10,1... | collective-permute-start | bytes 3128 | tf_op jit(solution)/shard_map/ppermute | solution.py:26
  198.4 6.6 %collective-permute-start.19 = (f32[2,130,1]{2,1,0:T(8,128)S(1)}, f32[2,130,1]{2,1,0:T(8,128)}, u32[]{:S(2)}, u32[]{:S(2)}) collective-permute-start(f32[2,130,1]{2,1,0:T(8,128)S(1)} %get-tuple-element.21), channel_id=1, source_target_pairs={{1,0},{2,1},{3,2},{0,3},{5,4},{6,5},{7,6},{4,7},{9,8},{10,9},{11,1... | collective-permute-start | bytes 3128 | tf_op jit(solution)/shard_map/ppermute | solution.py:28
  209.3 3.2 collective-permute-start.20
  212.7 6.4 %collective-permute-start.22 = (f32[2,130,1]{2,1,0:T(8,128)S(1)}, f32[2,130,1]{2,1,0:T(8,128)S(1)}, u32[]{:S(2)}, u32[]{:S(2)}) collective-permute-start(f32[2,130,1]{2,1,0:T(8,128)S(1)} %get-tuple-element.20), channel_id=1, source_target_pairs={{0,1},{1,2},{2,3},{3,0},{4,5},{5,6},{6,7},{7,4},{8,9},{9,10},{10,1... | collective-permute-start | bytes 3128 | tf_op jit(solution)/shard_map/ppermute | solution.py:26
  214.3 6.4 %collective-permute-start.23 = (f32[2,130,1]{2,1,0:T(8,128)S(1)}, f32[2,130,1]{2,1,0:T(8,128)}, u32[]{:S(2)}, u32[]{:S(2)}) collective-permute-start(f32[2,130,1]{2,1,0:T(8,128)S(1)} %get-tuple-element.19), channel_id=1, source_target_pairs={{1,0},{2,1},{3,2},{0,3},{5,4},{6,5},{7,6},{4,7},{9,8},{10,9},{11,1... | collective-permute-start | bytes 3128 | tf_op jit(solution)/shard_map/ppermute | solution.py:28
  225.0 3.2 collective-permute-start.24
  228.5 6.4 %collective-permute-start.26 = (f32[2,130,1]{2,1,0:T(8,128)S(1)}, f32[2,130,1]{2,1,0:T(8,128)S(1)}, u32[]{:S(2)}, u32[]{:S(2)}) collective-permute-start(f32[2,130,1]{2,1,0:T(8,128)S(1)} %get-tuple-element.18), channel_id=1, source_target_pairs={{0,1},{1,2},{2,3},{3,0},{4,5},{5,6},{6,7},{7,4},{8,9},{9,10},{10,1... | collective-permute-start | bytes 3128 | tf_op jit(solution)/shard_map/ppermute | solution.py:26
  229.9 6.4 %collective-permute-start.27 = (f32[2,130,1]{2,1,0:T(8,128)S(1)}, f32[2,130,1]{2,1,0:T(8,128)}, u32[]{:S(2)}, u32[]{:S(2)}) collective-permute-start(f32[2,130,1]{2,1,0:T(8,128)S(1)} %get-tuple-element.17), channel_id=1, source_target_pairs={{1,0},{2,1},{3,2},{0,3},{5,4},{6,5},{7,6},{4,7},{9,8},{10,9},{11,1... | collective-permute-start | bytes 3128 | tf_op jit(solution)/shard_map/ppermute | solution.py:28
  (28 other events, 233.0 us)
Sparse Core Ops, SparseCore 0:
  241.6 197.6 reduce-scatter.1
where the time goes:
time: 455 us; the launch traced here: 446 us
  waiting for transfers between devices  242 us (53%)
  blocking collectives  128 us (28%)
  starting transfers between devices  27.8 us (6%)
  other arithmetic  18.9 us (4%)
  between operations  17.1 us (4%)
  local copies, waits for them, and re-layouts  12.4 us (3%)
    reduce_scatter x1, waiting for transfers between devices, body(): return lax.psum_scatter(weighted, 'pole', scatter_dimension=0, tiled=True)  198 us
    all_gather x1, blocking collectives, body(): lax.all_gather(east_wind, 'pole', axis=0, tiled=True)  47.2 us
    all_gather x1, blocking collectives, body(): lax.all_gather(height, 'pole', axis=0, tiled=True)  42.3 us
    all_gather x1, blocking collectives, body(): lax.all_gather(north_wind, 'pole', axis=0, tiled=True)  38.8 us
    ppermute x14, waiting for transfers between devices, padded_2(): lax.ppermute(tail, axis, [(i, (i + 1) % count) for i in range(count)])  33.3 us
    ppermute x14, starting transfers between devices, padded_2(): lax.ppermute(head, axis, [((i + 1) % count, i) for i in range(count)])  16.2 us
    ppermute x14, starting transfers between devices, padded_2(): lax.ppermute(tail, axis, [(i, (i + 1) % count) for i in range(count)])  11.6 us
    ppermute x14, waiting for transfers between devices, padded_2(): lax.ppermute(head, axis, [((i + 1) % count, i) for i in range(count)])  10.8 us
  transfers between devices with their start and end apart: 29, of which 22 were waited for; matrix products, arithmetic and copies ran while one was open for 0% of the time, Pallas kernels for 0%

commit v1 on v0

v1 whole, which is shorter than its diff:
```python
import math

import jax
import jax.numpy as jnp
from jax import lax
from jax.experimental import pallas as pl
from jax.experimental.pallas import tpu as pltpu
from jax.sharding import PartitionSpec as P

coriolis_max = 1.0
zonal_coupling = 1.0
merid_coupling = 1.0
flux_scale = 0.5
north_scale = 0.25
relax_weights = (0.8, 1.0, 0.9, 1.0, 0.85, 1.0)

POLES = 16
LANES = 128
ROWS = 8
COLS = 1024
HALO = 6
TILES = 9
WIDE = TILES * LANES
STEP = LANES - 2 * HALO
F32 = jnp.float32

VMEM = pl.BlockSpec(memory_space=pltpu.VMEM)


def row_terms(row_index, total_rows):
    theta = math.pi * ((row_index + 0.5) / total_rows - 0.5)
    cosine = jnp.cos(theta)
    coriolis = coriolis_max * jnp.sin(theta)
    coriolis_sq = coriolis * coriolis
    zonal_coef = zonal_coupling / (cosine * cosine + 0.01)
    east_coef = flux_scale / (cosine + 0.05)
    return coriolis_sq, zonal_coef, east_coef


def near_depth(depth_ref, block, columns):
    last = depth_ref.shape[0] // ROWS - 1
    rows = [jnp.maximum(block - 1, 0), block, jnp.minimum(block + 1, last)]
    return [depth_ref[pl.ds(pl.multiple_of(r * ROWS, ROWS), ROWS), columns] for r in rows]


def edges_kernel(height, east, north, depth, to_right, to_left):
    block = lax.axis_index("pole")
    for out, first in ((to_right, COLS - LANES), (to_left, 0)):
        columns = slice(first, first + LANES)
        parts = [height[:, columns], east[:, columns], north[:, columns]]
        parts += near_depth(depth, block, columns)
        for i, part in enumerate(parts):
            out[i * ROWS : (i + 1) * ROWS, :] = part


def rows_kernel(height, east, north, depth, from_left, from_right, east_coef, field, winds, depths, send_near, send_far):
    block = lax.axis_index("pole")
    even = lax.rem(block, 2) == 0
    lane = lax.broadcasted_iota(jnp.int32, (ROWS, LANES), 1)
    row = lax.broadcasted_iota(jnp.int32, (ROWS, WIDE), 0)

    def widened(own, part):
        at = slice(part * ROWS, (part + 1) * ROWS)
        return jnp.concatenate([own, jnp.where(lane < LANES // 2, from_right[at, :], from_left[at, :])], axis=1)

    high = widened(height[...], 0)
    eastward = widened(east[...], 1)
    northward = widened(north[...], 2)
    coef = jnp.concatenate([east_coef[...]] * TILES, axis=1)
    partial = high - coef * (pltpu.roll(eastward, WIDE - 1, 1) - pltpu.roll(eastward, 1, 1))
    below = jnp.where(row == ROWS - 1, 0.0, pltpu.roll(northward, ROWS - 1, 0))
    above = jnp.where(row == 0, 0.0, pltpu.roll(northward, 1, 0))
    partial = partial - north_scale * (below - above)
    field[...] = partial
    winds[...] = northward
    upward = jnp.where(row < HALO, partial, pltpu.roll(northward, HALO, 0))
    downward = jnp.where(row < HALO, pltpu.roll(partial, ROWS - 2, 0), pltpu.roll(northward, ROWS - 1, 0))
    send_near[...] = jnp.where(even, downward, upward)
    send_far[0:ROWS, :] = jnp.where(even, upward, downward)
    for i, part in enumerate(near_depth(depth, block, slice(None))):
        part = widened(part, 3 + i)
        depths[i * ROWS : (i + 1) * ROWS, :] = part
        if i == 1:
            send_far[ROWS : 2 * ROWS, :] = part


def solve_kernel(field, winds, depths, near, far, table, coriolis, zonal, out, rhs_w, depth_w, base_w, zonal_w, gain, total, result):
    block = lax.axis_index("pole")
    band = lax.axis_index("lat")
    even = lax.rem(block, 2) == 0
    top = jnp.logical_and(band == 0, block == 0)
    last_block = lax.axis_size("pole") - 1
    bottom = jnp.logical_and(band == lax.axis_size("lat") - 1, block == last_block)
    row = lax.broadcasted_iota(jnp.int32, (ROWS, WIDE), 0)

    near_rows, far_rows, far_depth = near[...], far[0:ROWS, :], far[ROWS : 2 * ROWS, :]
    upper = jnp.where(top, 0.0, jnp.where(even, far_rows, near_rows))
    lower = jnp.where(bottom, 0.0, jnp.where(even, near_rows, far_rows))
    north = winds[...]
    from_above = north_scale * pltpu.roll(upper, ROWS - HALO, 0)
    from_below = north_scale * pltpu.roll(lower, 1, 0)
    mid = field[...] + jnp.where(row == 0, from_above, 0.0) - jnp.where(row == ROWS - 1, from_below, 0.0)
    own_first = jnp.where(top, 0.0, north_scale * pltpu.roll(north, ROWS - 1, 0))
    own_last = jnp.where(bottom, 0.0, north_scale * pltpu.roll(north, 1, 0))
    above = pltpu.roll(upper, ROWS - HALO, 0) - jnp.where(row == ROWS - 1, own_first, 0.0)
    below = lower + jnp.where(row == 0, own_last, 0.0)
    d_above = jnp.where(block == 0, far_depth, depths[0:ROWS, :])
    d_mid = depths[ROWS : 2 * ROWS, :]
    d_below = jnp.where(block == last_block, far_depth, depths[2 * ROWS : 3 * ROWS, :])

    def window(wide, t):
        first = t * STEP - HALO
        tile, shift = divmod(first, LANES)
        if tile < 0:
            pair = jnp.concatenate([wide[:, WIDE - LANES :], wide[:, :LANES]], axis=1)
        else:
            pair = wide[:, tile * LANES : (tile + 2) * LANES]
        return pltpu.roll(pair, 2 * LANES - shift, 1)[:, :LANES]

    for i, (rhs, deep) in enumerate(((above, d_above), (mid, d_mid), (below, d_below))):
        at = slice(i * ROWS, (i + 1) * ROWS)
        z = zonal[at, :]
        for t in range(TILES):
            d = window(deep, t)
            rhs_w[t, at, :] = window(rhs, t) / d
            depth_w[t, at, :] = d
            base_w[t, at, :] = coriolis[at, :] + 2.0 * d * (z + merid_coupling)
        zonal_w[at, :] = z

    sub = lax.broadcasted_iota(jnp.int32, (ROWS, LANES), 0)
    lane = lax.broadcasted_iota(jnp.int32, (ROWS, LANES), 1)
    numbers = jnp.broadcast_to(table[...] + near[ROWS - 1 : ROWS, 0:LANES], (ROWS, LANES))

    def number(which, group):
        picked = jnp.where(lane == which * POLES + group * ROWS + sub, numbers, 0.0)
        return jnp.broadcast_to(jnp.sum(picked, axis=1, keepdims=True), (ROWS, LANES))

    groups = POLES // ROWS
    params = [[number(which, g) for which in range(4)] for g in range(groups)]
    first, end = ROWS - HALO, 2 * ROWS + HALO

    def one_window(t, carry):
        sums = [jnp.zeros((ROWS, LANES), F32)] * ROWS
        for g in range(groups):
            real, imag, wreal, wimag = params[g]
            imag_sq = imag * imag
            p_real, p_imag = {}, {}
            for j in range(first, end):
                d = jnp.broadcast_to(depth_w[t, j : j + 1, :], (ROWS, LANES))
                if j < ROWS:
                    d = jnp.where(top, 0.0, d)
                if j >= 2 * ROWS:
                    d = jnp.where(bottom, 0.0, d)
                diag = real + jnp.broadcast_to(base_w[t, j : j + 1, :], (ROWS, LANES))
                scale = d / (diag * diag + imag_sq)
                g_real = scale * diag
                g_imag = -(scale * imag)
                gain[0, j] = g_real
                gain[1, j] = g_imag
                r = jnp.broadcast_to(rhs_w[t, j : j + 1, :], (ROWS, LANES))
                p_real[j] = r * g_real
                p_imag[j] = r * g_imag
            alpha = 1.0
            for m, w in enumerate(relax_weights):
                n_real, n_imag = {}, {}
                for j in range(first + m + 1, end - m - 1):
                    z = jnp.broadcast_to(zonal_w[j : j + 1, :], (ROWS, LANES))
                    r = jnp.broadcast_to(rhs_w[t, j : j + 1, :], (ROWS, LANES))
                    if alpha != 1.0:
                        r = r * (1.0 / alpha)
                    s_real = z * (pltpu.roll(p_real[j], 1, 1) + pltpu.roll(p_real[j], LANES - 1, 1))
                    s_real = r + s_real + (p_real[j - 1] + p_real[j + 1])
                    s_imag = z * (pltpu.roll(p_imag[j], 1, 1) + pltpu.roll(p_imag[j], LANES - 1, 1))
                    s_imag = s_imag + (p_imag[j - 1] + p_imag[j + 1])
                    g_real, g_imag = gain[0, j], gain[1, j]
                    u_real = s_real * g_real - s_imag * g_imag
                    u_imag = s_real * g_imag + s_imag * g_real
                    if w != 1.0:
                        u_real = u_real + ((1.0 - w) / w) * p_real[j]
                        u_imag = u_imag + ((1.0 - w) / w) * p_imag[j]
                    n_real[j], n_imag[j] = u_real, u_imag
                p_real, p_imag = n_real, n_imag
                alpha = alpha * w
            wreal, wimag = alpha * wreal, alpha * wimag
            for j in range(ROWS):
                sums[j] = sums[j] + (wreal * p_real[ROWS + j] - wimag * p_imag[ROWS + j])
        for j in range(ROWS):
            result[t, j : j + 1, :] = jnp.sum(sums[j], axis=0, keepdims=True)
        return carry

    lax.fori_loop(0, TILES, one_window, 0)

    for q in range(COLS // LANES):
        value = jnp.zeros((ROWS, LANES), F32)
        for t in range(TILES):
            begin, stop = max(t * STEP, q * LANES), min((t + 1) * STEP, (q + 1) * LANES)
            if begin < stop:
                shift = (t * STEP - HALO - q * LANES) % LANES
                moved = pltpu.roll(result[t], shift, 1) if shift else result[t]
                inside = jnp.logical_and(lane >= begin - q * LANES, lane < stop - q * LANES)
                value = jnp.where(inside, moved, value)
        out[:, q * LANES : (q + 1) * LANES] = value


def shape(*dims):
    return jax.ShapeDtypeStruct(dims, F32)


def call(kernel, outs, n_in, flops, scratch=()):
    return pl.pallas_call(
        kernel,
        out_shape=outs,
        in_specs=[VMEM] * n_in,
        out_specs=[VMEM] * len(outs),
        scratch_shapes=list(scratch),
        cost_estimate=pl.CostEstimate(flops=flops, bytes_accessed=200000, transcendentals=0),
        compiler_params=pltpu.CompilerParams(vmem_limit_bytes=32 * 1024 * 1024),
    )


def body(height, east_wind, north_wind, depth, pole_real, pole_imag, weight_real, weight_imag):
    n_pole, n_lat, n_lon = (lax.axis_size(a) for a in ("pole", "lat", "lon"))
    pole, lat = lax.axis_index("pole"), lax.axis_index("lat")
    total_rows = depth.shape[0] * n_lat
    first_row = (lat * n_pole + pole) * ROWS - ROWS
    rows = (first_row + lax.broadcasted_iota(jnp.int32, (3 * ROWS, LANES), 0)).astype(F32)
    coriolis, zonal, east_coef = row_terms(rows, total_rows)

    at = lax.broadcasted_iota(jnp.int32, (1, LANES), 1)
    table = jnp.zeros((1, LANES), F32)
    for i, value in enumerate((pole_real, pole_imag, weight_real, weight_imag)):
        table = jnp.where(at == i * POLES + pole, value[0], table)
    layers = n_pole // 2
    for partner in (lambda z: layers - 1 - z, lambda z: z ^ 2, lambda z: z ^ 1):
        pairs = [(2 * z + x, 2 * partner(z) + x) for z in range(layers) for x in range(2)]
        table = table + lax.ppermute(table, "pole", pairs)

    to_right, to_left = call(edges_kernel, [shape(6 * ROWS, LANES)] * 2, 4, 10000)(height, east_wind, north_wind, depth)
    from_left = lax.ppermute(to_right, "lon", [(i, (i + 1) % n_lon) for i in range(n_lon)])
    from_right = lax.ppermute(to_left, "lon", [((i + 1) % n_lon, i) for i in range(n_lon)])
    wide, both = shape(ROWS, WIDE), shape(2 * ROWS, WIDE)
    field, winds, depths, send_near, send_far = call(
        rows_kernel, [wide, wide, shape(3 * ROWS, WIDE), wide, both], 7, 100000
    )(height, east_wind, north_wind, depth, from_left, from_right, east_coef[ROWS : 2 * ROWS])

    total = n_lat * n_pole
    far_pairs = []
    for r in range(1, total, 2):
        for c in range(n_lon):
            one, two = (((b % n_pole) * n_lat + b // n_pole) * n_lon + c for b in (r, (r + 1) % total))
            far_pairs += [(one, two), (two, one)]
    far = lax.ppermute(send_far, ("pole", "lat", "lon"), far_pairs)
    send_near = lax.dynamic_update_slice(send_near, table, (ROWS - 1, 0))
    near = lax.ppermute(send_near, "pole", [(i, i ^ 1) for i in range(n_pole)])

    scratch = [
        pltpu.VMEM((TILES, 3 * ROWS, LANES), F32),
        pltpu.VMEM((TILES, 3 * ROWS, LANES), F32),
        pltpu.VMEM((TILES, 3 * ROWS, LANES), F32),
        pltpu.VMEM((3 * ROWS, LANES), F32),
        pltpu.VMEM((2, 3 * ROWS, ROWS, LANES), F32),
        pltpu.VMEM((ROWS, LANES), F32),
        pltpu.VMEM((TILES, ROWS, LANES), F32),
    ]
    (out,) = call(solve_kernel, [shape(ROWS, COLS)], 8, 60000000, scratch)(
        field, winds, depths, near, far, table, coriolis, zonal
    )
    return out


def solution(mesh):
    rows = P(("lat", "pole"), "lon")
    one = P("pole")
    in_specs = (rows, rows, rows, P("lat", "lon"), one, one, one, one)
    return jax.shard_map(body, mesh=mesh, in_specs=in_specs, out_specs=rows, check_vma=False)
```

time: 455 us -> 43.1 us (0.09)
  the two profiles are of different devices: /device:TPU:8 before, /device:TPU:32 now
where the time goes in v1:
time: 43.1 us; the launch traced here: 42.8 us
  waiting for transfers between devices  13.8 us (32%)
  starting transfers between devices  13.3 us (31%)
  Pallas kernels  9.79 us (23%)
  local copies, waits for them, and re-layouts  3.09 us (7%)
  between operations  2.66 us (6%)
    pallas_call x1, Pallas kernels, body(): call(solve_kernel, [shape(ROWS, COLS)], 8, 60000000, scratch)  9.68 us
    ppermute x3, waiting for transfers between devices, body(): table = table + lax.ppermute(table, 'pole', pairs)  7.18 us
    ppermute x3, starting transfers between devices, body(): table = table + lax.ppermute(table, 'pole', pairs)  6.77 us
    ppermute x1, waiting for transfers between devices, body(): far = lax.ppermute(send_far, ('pole', 'lat', 'lon'), far_pairs)  4.01 us
    ppermute x1, starting transfers between devices, body(): near = lax.ppermute(send_near, 'pole', [(i, i ^ 1) for i in range(n_pole)])  3.11 us
    ppermute x1, waiting for transfers between devices, body(): near = lax.ppermute(send_near, 'pole', [(i, i ^ 1) for i in range(n_pole)])  2.63 us
    unnamed x14, local copies, waits for them, and re-layouts  2.57 us
    ppermute x1, starting transfers between devices, body(): lax.ppermute(to_left, 'lon', [((i + 1) % n_lon, i) for i in range(n_lon)])  1.66 us
  transfers between devices with their start and end apart: 7, of which 4 were waited for; matrix products, arithmetic and copies ran while one was open for 0% of the time, Pallas kernels for 0%

profile of v1, /device:TPU:32, one launch (start us, length us, event | category | flops | bytes accessed | tf_op | source)
XLA Modules:
  0.0 42.8 jit_solution(12907994533226189948)
XLA Ops:
  2.6 5.9 %collective-permute-start.2 = (f32[1,128]{1,0:T(1,128)S(1)}, f32[1,128]{1,0:T(1,128)S(1)}, u32[]{:S(2)}, u32[]{:S(2)}) collective-permute-start(f32[1,128]{1,0:T(1,128)S(1)} %compare_select_fusion.3), channel_id=1, source_target_pairs={{0,224},{16,240},{32,192},{48,208},{64,160},{80,176},{96,128},{112... | collective-permute-start | bytes 1544 | tf_op jit(solution)/shard_map/ppermute | solution.py:236
  8.6 1.0 %copy-done = f32[128,1024]{1,0:T(8,128)S(1)} copy-done((f32[128,1024]{1,0:T(8,128)S(1)}, f32[128,1024]{1,0:T(8,128)}, u32[]{:S(2)}) %copy-start) | copy-done | bytes 524312
  9.6 0.8 %copy-done.3 = f32[8,1024]{1,0:T(8,128)S(1)} copy-done((f32[8,1024]{1,0:T(8,128)S(1)}, f32[8,1024]{1,0:T(8,128)}, u32[]{:S(2)}) %copy-start.3) | copy-done | bytes 32792
  10.4 0.8 %copy-done.5 = f32[8,1024]{1,0:T(8,128)S(1)} copy-done((f32[8,1024]{1,0:T(8,128)S(1)}, f32[8,1024]{1,0:T(8,128)}, u32[]{:S(2)}) %copy-start.5) | copy-done | bytes 32792
  11.1 0.0 copy-start.4
  11.1 1.7 %collective-permute-start = (f32[48,128]{1,0:T(8,128)S(1)}, f32[48,128]{1,0:T(8,128)S(1)}, u32[]{:S(2)}, u32[]{:S(2)}) collective-permute-start(f32[48,128]{1,0:T(8,128)S(1)} %get-tuple-element.12), channel_id=1, source_target_pairs={{0,1},{1,2},{2,3},{3,0},{4,5},{5,6},{6,7},{7,4},{8,9},{9,10},{10,1... | collective-permute-start | bytes 73736 | tf_op jit(solution)/shard_map/ppermute | solution.py:239
  12.8 1.7 %collective-permute-start.1 = (f32[48,128]{1,0:T(8,128)S(1)}, f32[48,128]{1,0:T(8,128)S(1)}, u32[]{:S(2)}, u32[]{:S(2)}) collective-permute-start(f32[48,128]{1,0:T(8,128)S(1)} %get-tuple-element.13), channel_id=1, source_target_pairs={{1,0},{2,1},{3,2},{0,3},{5,4},{6,5},{7,6},{4,7},{9,8},{10,9},{11,1... | collective-permute-start | bytes 73736 | tf_op jit(solution)/shard_map/ppermute | solution.py:240
  14.5 0.0 collective-permute-done.2
  14.5 0.6 %collective-permute-start.3 = (f32[1,128]{1,0:T(1,128)S(1)}, f32[1,128]{1,0:T(1,128)S(1)}, u32[]{:S(2)}, u32[]{:S(2)}) collective-permute-start(f32[1,128]{1,0:T(1,128)S(1)} %fusion.1), channel_id=1, source_target_pairs={{0,64},{16,80},{32,96},{48,112},{64,0},{80,16},{96,32},{112,48},{1... | collective-permute-start | bytes 1544 | tf_op jit(solution)/shard_map/ppermute | solution.py:236
  15.1 3.9 %collective-permute-done.3 = f32[1,128]{1,0:T(1,128)S(1)} collective-permute-done((f32[1,128]{1,0:T(1,128)S(1)}, f32[1,128]{1,0:T(1,128)S(1)}, u32[]{:S(2)}, u32[]{:S(2)}) %collective-permute-start.3) | collective-permute-done | bytes 544 | tf_op jit(solution)/shard_map/ppermute | solution.py:236
  19.0 0.2 collective-permute-start.4
  19.2 0.1 slice.4
  19.3 3.3 %collective-permute-done.4 = f32[1,128]{1,0:T(1,128)S(1)} collective-permute-done((f32[1,128]{1,0:T(1,128)S(1)}, f32[1,128]{1,0:T(1,128)S(1)}, u32[]{:S(2)}, u32[]{:S(2)}) %collective-permute-start.4) | collective-permute-done | bytes 544 | tf_op jit(solution)/shard_map/ppermute | solution.py:236
  22.6 0.0 collective-permute-done.from_left
  22.6 0.1 iota.22.east_coef
  22.7 0.1 shard_map.83
  22.8 0.2 dynamic_update_slice.3
  23.1 3.1 %collective-permute-start.5 = (f32[8,1152]{1,0:T(8,128)S(1)}, f32[8,1152]{1,0:T(8,128)S(1)}, u32[]{:S(2)}, u32[]{:S(2)}) collective-permute-start(f32[8,1152]{1,0:T(8,128)S(1)} %dynamic_update_slice.3), channel_id=1, source_target_pairs={{0,16},{16,0},{32,48},{48,32},{64,80},{80,64},{96,112},{112,96},{1... | collective-permute-start | bytes 110600 | tf_op jit(solution)/shard_map/ppermute | solution.py:254
  26.2 0.1 collective-permute-start.6
  26.3 2.6 %collective-permute-done.5.near = f32[8,1152]{1,0:T(8,128)S(1)} collective-permute-done((f32[8,1152]{1,0:T(8,128)S(1)}, f32[8,1152]{1,0:T(8,128)S(1)}, u32[]{:S(2)}, u32[]{:S(2)}) %collective-permute-start.5) | collective-permute-done | bytes 36896 | tf_op jit(solution)/shard_map/ppermute | solution.py:254
  28.9 4.0 %collective-permute-done.6.far = f32[16,1152]{1,0:T(8,128)S(1)} collective-permute-done((f32[16,1152]{1,0:T(8,128)S(1)}, f32[16,1152]{1,0:T(8,128)S(1)}, u32[]{:S(2)}, u32[]{:S(2)}) %collective-permute-start.6) | collective-permute-done | bytes 73760 | tf_op jit(solution)/shard_map/ppermute | solution.py:252
  32.9 0.1 iota.27.coriolis
  33.0 0.1 iota.28.zonal
  33.1 9.7 %shard_map.84 = f32[8,1024]{1,0:T(8,128)} custom-call(f32[8,1152]{1,0:T(8,128)S(1)} %get-tuple-element.14.field, f32[8,1152]{1,0:T(8,128)S(1)} %get-tuple-element.15.winds, f32[24,1152]{1,0:T(8,128)S(1)} %get-tuple-element.16.depths, f32[8,1152]{1,0:T(8,128)S(1)} %collective-permute-done.5.near, f32[16,1152]{1,0:T(8,128)S(1)} %collective-permute-done.6.far, ...), custom_call_target="tpu_custom_call" | custom-call | flops 60000000 | bytes 200000 | tf_op jit(solution)/shard_map/pallas_call | solution.py:265
  (18 shorter events, 0.1 us)
Async XLA Ops:
  0.0 8.6 %copy-start.2 = (f32[8,1024]{1,0:T(8,128)S(1)}, f32[8,1024]{1,0:T(8,128)}, u32[]{:S(2)}) copy-start(f32[8,1024]{1,0:T(8,128)} %height.3) | copy-start | bytes 98308
  2.6 11.8 %collective-permute-start.2 = (f32[1,128]{1,0:T(1,128)S(1)}, f32[1,128]{1,0:T(1,128)S(1)}, u32[]{:S(2)}, u32[]{:S(2)}) collective-permute-start(f32[1,128]{1,0:T(1,128)S(1)} %compare_select_fusion.3), channel_id=1, source_target_pairs={{0,224},{16,240},{32,192},{48,208},{64,160},{80,176},{96,128},{112... | collective-permute-start | bytes 1544 | tf_op jit(solution)/shard_map/ppermute | solution.py:236
  8.6 1.0 %copy-start = (f32[128,1024]{1,0:T(8,128)S(1)}, f32[128,1024]{1,0:T(8,128)}, u32[]{:S(2)}) copy-start(f32[128,1024]{1,0:T(8,128)} %depth.3) | copy-start | bytes 1572868
  9.6 0.8 %copy-start.3 = (f32[8,1024]{1,0:T(8,128)S(1)}, f32[8,1024]{1,0:T(8,128)}, u32[]{:S(2)}) copy-start(f32[8,1024]{1,0:T(8,128)} %east.3) | copy-start | bytes 98308
  10.4 0.8 %copy-start.5 = (f32[8,1024]{1,0:T(8,128)S(1)}, f32[8,1024]{1,0:T(8,128)}, u32[]{:S(2)}) copy-start(f32[8,1024]{1,0:T(8,128)} %north.3) | copy-start | bytes 98308
  11.1 11.6 %copy-start.1 = (f32[128,1024]{1,0:T(8,128)S(1)}, f32[128,1024]{1,0:T(8,128)}, u32[]{:S(2)}) copy-start(f32[128,1024]{1,0:T(8,128)} %depth.3) | copy-start | bytes 1572868
  11.1 11.6 %copy-start.6 = (f32[8,1024]{1,0:T(8,128)S(1)}, f32[8,1024]{1,0:T(8,128)}, u32[]{:S(2)}) copy-start(f32[8,1024]{1,0:T(8,128)} %north.3) | copy-start | bytes 98308
  11.1 11.6 %copy-start.4 = (f32[8,1024]{1,0:T(8,128)S(1)}, f32[8,1024]{1,0:T(8,128)}, u32[]{:S(2)}) copy-start(f32[8,1024]{1,0:T(8,128)} %east.3) | copy-start | bytes 98308
  11.1 11.5 %collective-permute-start = (f32[48,128]{1,0:T(8,128)S(1)}, f32[48,128]{1,0:T(8,128)S(1)}, u32[]{:S(2)}, u32[]{:S(2)}) collective-permute-start(f32[48,128]{1,0:T(8,128)S(1)} %get-tuple-element.12), channel_id=1, source_target_pairs={{0,1},{1,2},{2,3},{3,0},{4,5},{5,6},{6,7},{7,4},{8,9},{9,10},{10,1... | collective-permute-start | bytes 73736 | tf_op jit(solution)/shard_map/ppermute | solution.py:239
  12.8 9.8 %collective-permute-start.1 = (f32[48,128]{1,0:T(8,128)S(1)}, f32[48,128]{1,0:T(8,128)S(1)}, u32[]{:S(2)}, u32[]{:S(2)}) collective-permute-start(f32[48,128]{1,0:T(8,128)S(1)} %get-tuple-element.13), channel_id=1, source_target_pairs={{1,0},{2,1},{3,2},{0,3},{5,4},{6,5},{7,6},{4,7},{9,8},{10,9},{11,1... | collective-permute-start | bytes 73736 | tf_op jit(solution)/shard_map/ppermute | solution.py:240
  14.5 4.5 %collective-permute-start.3 = (f32[1,128]{1,0:T(1,128)S(1)}, f32[1,128]{1,0:T(1,128)S(1)}, u32[]{:S(2)}, u32[]{:S(2)}) collective-permute-start(f32[1,128]{1,0:T(1,128)S(1)} %fusion.1), channel_id=1, source_target_pairs={{0,64},{16,80},{32,96},{48,112},{64,0},{80,16},{96,32},{112,48},{1... | collective-permute-start | bytes 1544 | tf_op jit(solution)/shard_map/ppermute | solution.py:236
  19.0 3.6 %collective-permute-start.4 = (f32[1,128]{1,0:T(1,128)S(1)}, f32[1,128]{1,0:T(1,128)S(1)}, u32[]{:S(2)}, u32[]{:S(2)}) collective-permute-start(f32[1,128]{1,0:T(1,128)S(1)} %fusion.2), channel_id=1, source_target_pairs={{0,32},{16,48},{32,0},{48,16},{64,96},{80,112},{96,64},{112,80},{1... | collective-permute-start | bytes 1544 | tf_op jit(solution)/shard_map/ppermute | solution.py:236
  23.1 5.9 %collective-permute-start.5 = (f32[8,1152]{1,0:T(8,128)S(1)}, f32[8,1152]{1,0:T(8,128)S(1)}, u32[]{:S(2)}, u32[]{:S(2)}) collective-permute-start(f32[8,1152]{1,0:T(8,128)S(1)} %dynamic_update_slice.3), channel_id=1, source_target_pairs={{0,16},{16,0},{32,48},{48,32},{64,80},{80,64},{96,112},{112,96},{1... | collective-permute-start | bytes 110600 | tf_op jit(solution)/shard_map/ppermute | solution.py:254
  26.2 6.8 %collective-permute-start.6 = (f32[16,1152]{1,0:T(8,128)S(1)}, f32[16,1152]{1,0:T(8,128)S(1)}, u32[]{:S(2)}, u32[]{:S(2)}) collective-permute-start(f32[16,1152]{1,0:T(8,128)S(1)} %get-tuple-element.18), channel_id=1, source_target_pairs={{16,32},{32,16},{17,33},{33,17},{18,34},{34,18},{19,35},{35,19},{4... | collective-permute-start | bytes 221192 | tf_op jit(solution)/shard_map/ppermute | solution.py:252

commit v2 on v1

v2 whole, which is shorter than its diff:
```python
import math

import jax
import jax.numpy as jnp
from jax import lax
from jax.experimental import pallas as pl
from jax.experimental.pallas import tpu as pltpu
from jax.sharding import PartitionSpec as P

coriolis_max = 1.0
zonal_coupling = 1.0
merid_coupling = 1.0
flux_scale = 0.5
north_scale = 0.25
relax_weights = (0.8, 1.0, 0.9, 1.0, 0.85, 1.0)

POLES = 16
LANES = 128
ROWS = 8
COLS = 1024
HALO = 6
TILES = 9
WIDE = TILES * LANES
INVERSE = pow(TILES, -1, LANES)
F32 = jnp.float32
LIMIT = 24 * 1024 * 1024

VMEM = pl.BlockSpec(memory_space=pltpu.VMEM)


def row_terms(row_index, total_rows):
    theta = math.pi * ((row_index + 0.5) / total_rows - 0.5)
    cosine = jnp.cos(theta)
    coriolis = coriolis_max * jnp.sin(theta)
    coriolis_sq = coriolis * coriolis
    zonal_coef = zonal_coupling / (cosine * cosine + 0.01)
    east_coef = flux_scale / (cosine + 0.05)
    return coriolis_sq, zonal_coef, east_coef


def near_depth(depth_at, block, depth_rows, columns):
    last = depth_rows // ROWS - 1
    rows = [jnp.maximum(block - 1, 0), block, jnp.minimum(block + 1, last)]
    return [depth_at[pl.ds(pl.multiple_of(r * ROWS, ROWS), ROWS), columns] for r in rows]


def edges_kernel(height, east, north, depth, to_right, to_left, around, sems):
    block = lax.axis_index("pole")
    copies = []
    for out, first in ((to_right, COLS - LANES), (to_left, 0)):
        columns = pl.ds(first, LANES)
        parts = [height.at[:, columns], east.at[:, columns], north.at[:, columns]]
        parts += near_depth(depth.at, block, depth.shape[0], columns)
        copies += [(part, out.at[pl.ds(i * ROWS, ROWS), :]) for i, part in enumerate(parts)]
    parts = near_depth(depth.at, block, depth.shape[0], pl.ds(0, COLS))
    copies += [(part, around.at[pl.ds(i * ROWS, ROWS), :]) for i, part in enumerate(parts)]
    copies = [pltpu.make_async_copy(source, target, sems.at[i]) for i, (source, target) in enumerate(copies)]
    for copy in copies:
        copy.start()
    for copy in copies:
        copy.wait()


def near_kernel(rows, one, two, after, out):
    out[0 : ROWS - 1, :] = rows[0 : ROWS - 1, :]
    out[ROWS - 1 : ROWS, 0:LANES] = one[...] + two[...]
    out[ROWS - 1 : ROWS, LANES:] = rows[ROWS - 1 : ROWS, LANES:]


def rows_kernel(height, east, north, around, from_left, from_right, after, field, winds, depths, send_near, send_far, coriolis, zonal):
    block, band = lax.axis_index("pole"), lax.axis_index("lat")
    total_rows = lax.axis_size("lat") * lax.axis_size("pole") * ROWS
    first_row = (band * lax.axis_size("pole") + block) * ROWS - ROWS
    index = (first_row + lax.broadcasted_iota(jnp.int32, (3 * ROWS, LANES), 0)).astype(F32)
    coriolis[...], zonal[...], east_coef = row_terms(index, total_rows)
    east_coef = east_coef[ROWS : 2 * ROWS, :]
    even = lax.rem(block, 2) == 0
    lane = lax.broadcasted_iota(jnp.int32, (ROWS, LANES), 1)
    row = lax.broadcasted_iota(jnp.int32, (ROWS, WIDE), 0)

    def widened(own, part):
        at = slice(part * ROWS, (part + 1) * ROWS)
        return jnp.concatenate([own, jnp.where(lane < LANES // 2, from_right[at, :], from_left[at, :])], axis=1)

    high = widened(height[...], 0)
    eastward = widened(east[...], 1)
    northward = widened(north[...], 2)
    coef = jnp.concatenate([east_coef] * TILES, axis=1)
    partial = high - coef * (pltpu.roll(eastward, WIDE - 1, 1) - pltpu.roll(eastward, 1, 1))
    below = jnp.where(row == ROWS - 1, 0.0, pltpu.roll(northward, ROWS - 1, 0))
    above = jnp.where(row == 0, 0.0, pltpu.roll(northward, 1, 0))
    partial = partial - north_scale * (below - above)
    field[...] = partial
    winds[...] = northward
    upward = jnp.where(row < HALO, partial, pltpu.roll(northward, HALO, 0))
    downward = jnp.where(row < HALO, pltpu.roll(partial, ROWS - 2, 0), pltpu.roll(northward, ROWS - 1, 0))
    send_near[...] = jnp.where(even, downward, upward)
    send_far[0:ROWS, :] = jnp.where(even, upward, downward)
    for i in range(3):
        part = widened(around[i * ROWS : (i + 1) * ROWS, :], 3 + i)
        depths[i * ROWS : (i + 1) * ROWS, :] = part
        if i == 1:
            send_far[ROWS : 2 * ROWS, :] = part


def solve_kernel(field, winds, depths, near, far, one, two, coriolis, zonal, out, rhs_w, depth_w, base_w, poles, gain, even_p, odd_p, result):
    block = lax.axis_index("pole")
    band = lax.axis_index("lat")
    even = lax.rem(block, 2) == 0
    top = jnp.logical_and(band == 0, block == 0)
    last_block = lax.axis_size("pole") - 1
    bottom = jnp.logical_and(band == lax.axis_size("lat") - 1, block == last_block)
    row = lax.broadcasted_iota(jnp.int32, (ROWS, WIDE), 0)

    near_rows, far_rows, far_depth = near[...], far[0:ROWS, :], far[ROWS : 2 * ROWS, :]
    upper = jnp.where(top, 0.0, jnp.where(even, far_rows, near_rows))
    lower = jnp.where(bottom, 0.0, jnp.where(even, near_rows, far_rows))
    north = winds[...]
    from_above = north_scale * pltpu.roll(upper, ROWS - HALO, 0)
    from_below = north_scale * pltpu.roll(lower, 1, 0)
    mid = field[...] + jnp.where(row == 0, from_above, 0.0) - jnp.where(row == ROWS - 1, from_below, 0.0)
    own_first = jnp.where(top, 0.0, north_scale * pltpu.roll(north, ROWS - 1, 0))
    own_last = jnp.where(bottom, 0.0, north_scale * pltpu.roll(north, 1, 0))
    above = pltpu.roll(upper, ROWS - HALO, 0) - jnp.where(row == ROWS - 1, own_first, 0.0)
    below = lower + jnp.where(row == 0, own_last, 0.0)
    d_above = jnp.where(block == 0, far_depth, depths[0:ROWS, :])
    d_mid = depths[ROWS : 2 * ROWS, :]
    d_below = jnp.where(block == last_block, far_depth, depths[2 * ROWS : 3 * ROWS, :])

    lane = lax.broadcasted_iota(jnp.int32, (ROWS, LANES), 1)
    sub = lax.broadcasted_iota(jnp.int32, (ROWS, LANES), 0)

    def owner(tile):
        return lax.rem(tile * LANES + lane, TILES)

    def dealt(wide, t):
        value = wide[:, 0:LANES]
        for q in range(1, TILES):
            value = jnp.where(owner(q) == t, wide[:, q * LANES : (q + 1) * LANES], value)
        return jnp.take_along_axis(value, lax.rem(lane * TILES + t, LANES), axis=1)

    for i, (rhs, deep) in enumerate(((above, d_above), (mid, d_mid), (below, d_below))):
        at = slice(i * ROWS, (i + 1) * ROWS)
        z = zonal[at, :]
        for t in range(TILES):
            d = dealt(deep, t)
            rhs_w[t, at, :] = dealt(rhs, t) / d
            base_w[t, at, :] = coriolis[at, :] + 2.0 * d * (z + merid_coupling)
            if i == 0:
                d = jnp.where(top, 0.0, d)
            if i == 2:
                d = jnp.where(bottom, 0.0, d)
            depth_w[t, at, :] = d

    numbers = jnp.broadcast_to((one[...] + two[...]) + near[ROWS - 1 : ROWS, 0:LANES], (ROWS, LANES))
    groups = POLES // ROWS
    for g in range(groups):
        for which in range(4):
            picked = jnp.where(lane == which * POLES + g * ROWS + sub, numbers, 0.0)
            poles[g, which] = jnp.broadcast_to(jnp.sum(picked, axis=1, keepdims=True), (ROWS, LANES))
    first, end = ROWS - HALO, 2 * ROWS + HALO

    def spread(ref, j, *index):
        return jnp.broadcast_to(ref[(*index, slice(j, j + 1), slice(None))], (ROWS, LANES))

    def begin(i, carry):
        g, t = i // TILES, lax.rem(i, TILES)
        real, imag = poles[g, 0], poles[g, 1]
        imag_sq = imag * imag
        for j in range(first, end):
            diag = real + spread(base_w, j, t)
            scale = spread(depth_w, j, t) / (diag * diag + imag_sq)
            g_real, g_imag = scale * diag, -(scale * imag)
            gain[g, 0, j, t] = g_real
            gain[g, 1, j, t] = g_imag
            r = spread(rhs_w, j, t)
            even_p[g, 0, j, t] = r * g_real
            even_p[g, 1, j, t] = r * g_imag
        return carry

    lax.fori_loop(0, groups * TILES, begin, 0)
    alpha = 1.0
    for m, w in enumerate(relax_weights):
        old, new = (even_p, odd_p) if m % 2 == 0 else (odd_p, even_p)
        low, high = first + m + 1, end - m - 1
        last = m == len(relax_weights) - 1

        def one_row(g, j):
            z = jnp.broadcast_to(zonal[pl.ds(j, 1), :], (ROWS, LANES))
            here = [[old[g, c, j, t] for t in range(TILES)] for c in range(2)]
            west = [pltpu.roll(here[c][TILES - 1], 1, 1) for c in range(2)]
            east = [pltpu.roll(here[c][0], LANES - 1, 1) for c in range(2)]
            for t in range(TILES):
                s_real, s_imag = (
                    z * ((here[c][t - 1] if t else west[c]) + (here[c][t + 1] if t < TILES - 1 else east[c]))
                    + (old[g, c, j - 1, t] + old[g, c, j + 1, t])
                    for c in range(2)
                )
                s_real = s_real + jnp.broadcast_to(rhs_w[t, pl.ds(j, 1), :], (ROWS, LANES))
                g_real, g_imag = gain[g, 0, j, t], gain[g, 1, j, t]
                u_real = s_real * g_real - s_imag * g_imag
                u_imag = s_real * g_imag + s_imag * g_real
                if w != 1.0:
                    u_real = u_real + ((1.0 - w) / w) * here[0][t]
                    u_imag = u_imag + ((1.0 - w) / w) * here[1][t]
                if last:
                    wreal, wimag = alpha * poles[g, 2], alpha * poles[g, 3]
                    value = jnp.sum(wreal * u_real - wimag * u_imag, axis=0, keepdims=True)
                    result[g, t, pl.ds(j - ROWS, 1), :] = value
                else:
                    new[g, 0, j, t] = u_real
                    new[g, 1, j, t] = u_imag

        def sweep(i, carry):
            for g in range(groups):
                for k in range(2):
                    one_row(g, low + 2 * i + k)
            return carry

        lax.fori_loop(0, (high - low) // 2, sweep, 0)
        if w != 1.0:
            alpha = alpha * w
            rhs_w[...] = rhs_w[...] * (1.0 / w)

    undealt = []
    for t in range(TILES):
        value = result[0, t]
        for g in range(1, groups):
            value = value + result[g, t]
        index = lax.rem((lane - t + LANES) * INVERSE, LANES)
        undealt.append(jnp.take_along_axis(value, index, axis=1))
    for q in range(COLS // LANES):
        value = undealt[0]
        for t in range(1, TILES):
            value = jnp.where(owner(q) == t, undealt[t], value)
        out[:, q * LANES : (q + 1) * LANES] = value


def shape(*dims):
    return jax.ShapeDtypeStruct(dims, F32)


def call(kernel, outs, n_in, flops, scratch=()):
    return pl.pallas_call(
        kernel,
        out_shape=outs,
        in_specs=[VMEM] * n_in,
        out_specs=[VMEM] * len(outs),
        scratch_shapes=list(scratch),
        cost_estimate=pl.CostEstimate(flops=flops, bytes_accessed=200000, transcendentals=0),
        compiler_params=pltpu.CompilerParams(vmem_limit_bytes=LIMIT),
    )


def body(height, east_wind, north_wind, depth, pole_real, pole_imag, weight_real, weight_imag):
    n_pole, n_lat, n_lon = (lax.axis_size(a) for a in ("pole", "lat", "lon"))
    pole = lax.axis_index("pole")
    at = lax.broadcasted_iota(jnp.int32, (1, LANES), 1)
    table = jnp.zeros((1, LANES), F32)
    for i, value in enumerate((pole_real, pole_imag, weight_real, weight_imag)):
        table = jnp.where(at == i * POLES + pole, value[0], table)
    layers = n_pole // 2

    def swapped(table, partner):
        pairs = [(2 * z + x, 2 * partner(z) + x) for z in range(layers) for x in range(2)]
        return lax.ppermute(table, "pole", pairs)

    table = first = (table + swapped(table, lambda z: layers - 1 - z))[0:1]
    table = table + swapped(table, lambda z: z ^ 2)
    third = swapped(table, lambda z: z ^ 1)

    column = shape(6 * ROWS, LANES)
    to_right, to_left, around = pl.pallas_call(
        edges_kernel,
        out_shape=[column, column, shape(3 * ROWS, COLS)],
        in_specs=[pl.BlockSpec(memory_space=pl.ANY)] * 4,
        out_specs=[VMEM] * 3,
        scratch_shapes=[pltpu.SemaphoreType.DMA((15,))],
        compiler_params=pltpu.CompilerParams(vmem_limit_bytes=66600000),
    )(height, east_wind, north_wind, depth)
    from_left = lax.ppermute(to_right, "lon", [(i, (i + 1) % n_lon) for i in range(n_lon)])
    from_right = lax.ppermute(to_left, "lon", [((i + 1) % n_lon, i) for i in range(n_lon)])
    wide, both = shape(ROWS, WIDE), shape(2 * ROWS, WIDE)
    terms = shape(3 * ROWS, LANES)
    field, winds, depths, send_near, send_far, coriolis, zonal = call(
        rows_kernel, [wide, wide, shape(3 * ROWS, WIDE), wide, both, terms, terms], 7, 100000
    )(height, east_wind, north_wind, around, from_left, from_right, first)

    total = n_lat * n_pole
    far_pairs = []
    for r in range(1, total, 2):
        for c in range(n_lon):
            one, two = (((b % n_pole) * n_lat + b // n_pole) * n_lon + c for b in (r, (r + 1) % total))
            far_pairs += [(one, two), (two, one)]
    far = lax.ppermute(send_far, ("pole", "lat", "lon"), far_pairs)
    (send_near,) = pl.pallas_call(
        near_kernel,
        out_shape=[wide],
        in_specs=[VMEM, VMEM, VMEM, pl.BlockSpec(memory_space=pl.ANY)],
        out_specs=[VMEM],
        compiler_params=pltpu.CompilerParams(vmem_limit_bytes=LIMIT),
    )(send_near, table, third, first)
    near = lax.ppermute(send_near, "pole", [(i, i ^ 1) for i in range(n_pole)])

    groups = POLES // ROWS
    tiles = pltpu.VMEM((TILES, 3 * ROWS, LANES), F32)
    iterate = pltpu.VMEM((groups, 2, 3 * ROWS, TILES, ROWS, LANES), F32)
    scratch = [
        tiles,
        tiles,
        tiles,
        pltpu.VMEM((groups, 4, ROWS, LANES), F32),
        pltpu.VMEM((groups, 2, 3 * ROWS, TILES, ROWS, LANES), F32),
        iterate,
        iterate,
        pltpu.VMEM((groups, TILES, ROWS, LANES), F32),
    ]
    (out,) = call(solve_kernel, [shape(ROWS, COLS)], 9, 60000000, scratch)(
        field, winds, depths, near, far, table, third, coriolis, zonal
    )
    return out


def solution(mesh):
    rows = P(("lat", "pole"), "lon")
    one = P("pole")
    in_specs = (rows, rows, rows, P("lat", "lon"), one, one, one, one)
    return jax.shard_map(body, mesh=mesh, in_specs=in_specs, out_specs=rows, check_vma=False)
```

time: 43.1 us -> 35.8 us (0.83)
  waiting for transfers between devices: 13.8 us -> 9.31 us
  local copies, waits for them, and re-layouts: 3.09 us -> 0.9 us
  Pallas kernels: 9.79 us -> 8.09 us
  starting transfers between devices: 13.3 us -> 14.1 us
    ppermute x1, waiting for transfers between devices: 4.01 us -> 0.01 us  [body(): far = lax.ppermute(send_far, ('pole', 'lat', 'lon'), far_pairs)]
    ppermute x3, waiting for transfers between devices: 7.18 us -> 3.53 us  [swapped(): return lax.ppermute(table, 'pole', pairs)]
    ppermute x1, starting transfers between devices: 0.06 us -> 2.76 us  [body(): far = lax.ppermute(send_far, ('pole', 'lat', 'lon'), far_pairs)]
    ppermute x1, starting transfers between devices: 3.11 us -> 1.41 us  [body(): near = lax.ppermute(send_near, 'pole', [(i, i ^ 1) for i in range(n_pole)])]
    pallas_call x3 -> x4, Pallas kernels: 9.79 us -> 8.09 us  [the longest x1 6.27 us: body(): call(solve_kernel, [shape(ROWS, COLS)], 9, 60000000, scratch)]
    unnamed x14 -> x8, local copies, waits for them, and re-layouts: 2.57 us -> 0.9 us
    ppermute x1, waiting for transfers between devices: 2.63 us -> 4.05 us  [body(): near = lax.ppermute(send_near, 'pole', [(i, i ^ 1) for i in range(n_pole)])]
    ppermute x1, waiting for transfers between devices: 0.01 us -> 1.36 us  [body(): lax.ppermute(to_right, 'lon', [(i, (i + 1) % n_lon) for i in range(n_lon)])]
  transfers between devices with their start and end apart: 7 -> 7, of which waited for: 4 -> 4; matrix products, arithmetic and copies ran while one was open for 0% -> 0% of each run, Pallas kernels for 0% -> 5%
where the time goes in v2:
time: 35.8 us; the launch traced here: 35.1 us
  starting transfers between devices  14.1 us (39%)
  waiting for transfers between devices  9.31 us (26%)
  Pallas kernels  8.09 us (23%)
  between operations  2.64 us (7%)
  local copies, waits for them, and re-layouts  0.9 us (3%)
    ppermute x3, starting transfers between devices, swapped(): return lax.ppermute(table, 'pole', pairs)  6.66 us
    pallas_call x1, Pallas kernels, body(): call(solve_kernel, [shape(ROWS, COLS)], 9, 60000000, scratch)  6.27 us
    ppermute x1, waiting for transfers between devices, body(): near = lax.ppermute(send_near, 'pole', [(i, i ^ 1) for i in range(n_pole)])  4.05 us
    ppermute x3, waiting for transfers between devices, swapped(): return lax.ppermute(table, 'pole', pairs)  3.53 us
    ppermute x1, starting transfers between devices, body(): far = lax.ppermute(send_far, ('pole', 'lat', 'lon'), far_pairs)  2.76 us
    pallas_call x1, Pallas kernels, body(): pl.pallas_call(edges_kernel, out_shape=[column, column, shape(3 * ROWS, C...  1.73 us
    ppermute x1, starting transfers between devices, body(): lax.ppermute(to_left, 'lon', [((i + 1) % n_lon, i) for i in range(n_lon)])  1.66 us
    ppermute x1, starting transfers between devices, body(): lax.ppermute(to_right, 'lon', [(i, (i + 1) % n_lon) for i in range(n_lon)])  1.65 us
  transfers between devices with their start and end apart: 7, of which 4 were waited for; matrix products, arithmetic and copies ran while one was open for 0% of the time, Pallas kernels for 5%

profile of v2, /device:TPU:32, one launch (start us, length us, event | category | flops | bytes accessed | tf_op | source)
XLA Modules:
  0.0 35.1 jit_solution(11298814431867785802)
XLA Ops:
  2.6 5.9 %collective-permute-start.2 = (f32[1,128]{1,0:T(1,128)S(1)}, f32[1,128]{1,0:T(1,128)S(1)}, u32[]{:S(2)}, u32[]{:S(2)}) collective-permute-start(f32[1,128]{1,0:T(1,128)S(1)} %compare_select_fusion.3), channel_id=1, source_target_pairs={{0,224},{16,240},{32,192},{48,208},{64,160},{80,176},{96,128},{112... | collective-permute-start | bytes 1544 | tf_op jit(solution)/shard_map/ppermute | solution.py:266
  8.5 0.0 copy-start
  8.5 0.0 copy-start.1
  8.5 1.7 %shard_map.82 = (f32[48,128]{1,0:T(8,128)}, f32[48,128]{1,0:T(8,128)}, f32[24,1024]{1,0:T(8,128)}) custom-call(f32[8,1024]{1,0:T(8,128)} %height.3, f32[8,1024]{1,0:T(8,128)} %east.3, f32[8,1024]{1,0:T(8,128)} %north.3, f32[128,1024]{1,0:T(8,128)} %depth.1), custom_call_target="tpu_custom_call" | custom-call | tf_op jit(solution)/shard_map/pallas_call | solution.py:273
  10.3 1.7 %collective-permute-start = (f32[48,128]{1,0:T(8,128)}, f32[48,128]{1,0:T(8,128)S(1)}, u32[]{:S(2)}, u32[]{:S(2)}) collective-permute-start(f32[48,128]{1,0:T(8,128)} %get-tuple-element.16), channel_id=1, source_target_pairs={{0,1},{1,2},{2,3},{3,0},{4,5},{5,6},{6,7},{7,4},{8,9},{9,10},{10,1... | collective-permute-start | bytes 73736 | tf_op jit(solution)/shard_map/ppermute | solution.py:281
  11.9 1.7 %collective-permute-start.1 = (f32[48,128]{1,0:T(8,128)}, f32[48,128]{1,0:T(8,128)S(1)}, u32[]{:S(2)}, u32[]{:S(2)}) collective-permute-start(f32[48,128]{1,0:T(8,128)} %get-tuple-element.17), channel_id=1, source_target_pairs={{1,0},{2,1},{3,2},{0,3},{5,4},{6,5},{7,6},{4,7},{9,8},{10,9},{11,1... | collective-permute-start | bytes 73736 | tf_op jit(solution)/shard_map/ppermute | solution.py:282
  13.6 0.0 collective-permute-done.2
  13.6 0.6 %collective-permute-start.3 = (f32[1,128]{1,0:T(1,128)S(1)}, f32[1,128]{1,0:T(1,128)S(1)}, u32[]{:S(2)}, u32[]{:S(2)}) collective-permute-start(f32[1,128]{1,0:T(1,128)S(1)} %fusion.after), channel_id=1, source_target_pairs={{0,64},{16,80},{32,96},{48,112},{64,0},{80,16},{96,32},{112,48},{1... | collective-permute-start | bytes 1544 | tf_op jit(solution)/shard_map/ppermute | solution.py:266
  14.2 1.4 %collective-permute-done.from_left = f32[48,128]{1,0:T(8,128)S(1)} collective-permute-done((f32[48,128]{1,0:T(8,128)}, f32[48,128]{1,0:T(8,128)S(1)}, u32[]{:S(2)}, u32[]{:S(2)}) %collective-permute-start) | collective-permute-done | bytes 24608 | tf_op jit(solution)/shard_map/ppermute | solution.py:281
  15.6 0.4 %collective-permute-done.1.from_right = f32[48,128]{1,0:T(8,128)S(1)} collective-permute-done((f32[48,128]{1,0:T(8,128)}, f32[48,128]{1,0:T(8,128)S(1)}, u32[]{:S(2)}, u32[]{:S(2)}) %collective-permute-start.1) | collective-permute-done | bytes 24608 | tf_op jit(solution)/shard_map/ppermute | solution.py:282
  16.0 0.0 copy-done
  16.0 0.0 copy-done.1
  16.0 0.0 copy-done.2
  16.0 0.0 copy-start.3
  16.0 0.9 %copy-done.3 = f32[24,1024]{1,0:T(8,128)S(1)} copy-done((f32[24,1024]{1,0:T(8,128)S(1)}, f32[24,1024]{1,0:T(8,128)}, u32[]{:S(2)}) %copy-start.3) | copy-done | bytes 98328
  16.9 0.1 shard_map.83
  17.0 2.8 %collective-permute-start.6 = (f32[16,1152]{1,0:T(8,128)S(1)}, f32[16,1152]{1,0:T(8,128)S(1)}, u32[]{:S(2)}, u32[]{:S(2)}) collective-permute-start(f32[16,1152]{1,0:T(8,128)S(1)} %get-tuple-element.22), channel_id=1, source_target_pairs={{16,32},{32,16},{17,33},{33,17},{18,34},{34,18},{19,35},{35,19},{4... | collective-permute-start | bytes 221192 | tf_op jit(solution)/shard_map/ppermute | solution.py:295
  19.7 0.0 collective-permute-done.3
  19.7 0.1 collective-permute-start.4
  19.8 3.5 %collective-permute-done.4.two = f32[1,128]{1,0:T(1,128)S(1)} collective-permute-done((f32[1,128]{1,0:T(1,128)S(1)}, f32[1,128]{1,0:T(1,128)S(1)}, u32[]{:S(2)}, u32[]{:S(2)}) %collective-permute-start.4) | collective-permute-done | bytes 544 | tf_op jit(solution)/shard_map/ppermute | solution.py:266
  23.4 1.4 %collective-permute-start.5 = (f32[8,1152]{1,0:T(8,128)S(1)}, f32[8,1152]{1,0:T(8,128)S(1)}, u32[]{:S(2)}, u32[]{:S(2)}) collective-permute-start(f32[8,1152]{1,0:T(8,128)S(1)} %shard_map.84), channel_id=1, source_target_pairs={{0,16},{16,0},{32,48},{48,32},{64,80},{80,64},{96,112},{112,96},{1... | collective-permute-start | bytes 110600 | tf_op jit(solution)/shard_map/ppermute | solution.py:303
  24.8 4.1 %collective-permute-done.5.near = f32[8,1152]{1,0:T(8,128)S(1)} collective-permute-done((f32[8,1152]{1,0:T(8,128)S(1)}, f32[8,1152]{1,0:T(8,128)S(1)}, u32[]{:S(2)}, u32[]{:S(2)}) %collective-permute-start.5) | collective-permute-done | bytes 36896 | tf_op jit(solution)/shard_map/ppermute | solution.py:303
  28.8 0.0 collective-permute-done.6.far
  28.9 6.3 %shard_map.85 = f32[8,1024]{1,0:T(8,128)} custom-call(f32[8,1152]{1,0:T(8,128)S(1)} %get-tuple-element.18.field, f32[8,1152]{1,0:T(8,128)S(1)} %get-tuple-element.19.winds, f32[24,1152]{1,0:T(8,128)S(1)} %get-tuple-element.20.depths, f32[8,1152]{1,0:T(8,128)S(1)} %collective-permute-done.5.near, f32[16,1152]{1,0:T(8,128)S(1)} %collective-permute-done.6.far, ...), custom_call_target="tpu_custom_call" | custom-call | flops 60000000 | bytes 200000 | tf_op jit(solution)/shard_map/pallas_call | solution.py:318
  (5 shorter events, 0.0 us)
Async XLA Ops:
  2.6 11.0 %collective-permute-start.2 = (f32[1,128]{1,0:T(1,128)S(1)}, f32[1,128]{1,0:T(1,128)S(1)}, u32[]{:S(2)}, u32[]{:S(2)}) collective-permute-start(f32[1,128]{1,0:T(1,128)S(1)} %compare_select_fusion.3), channel_id=1, source_target_pairs={{0,224},{16,240},{32,192},{48,208},{64,160},{80,176},{96,128},{112... | collective-permute-start | bytes 1544 | tf_op jit(solution)/shard_map/ppermute | solution.py:266
  8.5 7.4 %copy-start = (f32[8,1024]{1,0:T(8,128)S(1)}, f32[8,1024]{1,0:T(8,128)}, u32[]{:S(2)}) copy-start(f32[8,1024]{1,0:T(8,128)} %height.3) | copy-start | bytes 98308
  8.5 7.4 %copy-start.1 = (f32[8,1024]{1,0:T(8,128)S(1)}, f32[8,1024]{1,0:T(8,128)}, u32[]{:S(2)}) copy-start(f32[8,1024]{1,0:T(8,128)} %east.3) | copy-start | bytes 98308
  8.5 7.4 %copy-start.2 = (f32[8,1024]{1,0:T(8,128)S(1)}, f32[8,1024]{1,0:T(8,128)}, u32[]{:S(2)}) copy-start(f32[8,1024]{1,0:T(8,128)} %north.3) | copy-start | bytes 98308
  10.3 5.3 %collective-permute-start = (f32[48,128]{1,0:T(8,128)}, f32[48,128]{1,0:T(8,128)S(1)}, u32[]{:S(2)}, u32[]{:S(2)}) collective-permute-start(f32[48,128]{1,0:T(8,128)} %get-tuple-element.16), channel_id=1, source_target_pairs={{0,1},{1,2},{2,3},{3,0},{4,5},{5,6},{6,7},{7,4},{8,9},{9,10},{10,1... | collective-permute-start | bytes 73736 | tf_op jit(solution)/shard_map/ppermute | solution.py:281
  11.9 4.0 %collective-permute-start.1 = (f32[48,128]{1,0:T(8,128)}, f32[48,128]{1,0:T(8,128)S(1)}, u32[]{:S(2)}, u32[]{:S(2)}) collective-permute-start(f32[48,128]{1,0:T(8,128)} %get-tuple-element.17), channel_id=1, source_target_pairs={{1,0},{2,1},{3,2},{0,3},{5,4},{6,5},{7,6},{4,7},{9,8},{10,9},{11,1... | collective-permute-start | bytes 73736 | tf_op jit(solution)/shard_map/ppermute | solution.py:282
  13.6 6.1 %collective-permute-start.3 = (f32[1,128]{1,0:T(1,128)S(1)}, f32[1,128]{1,0:T(1,128)S(1)}, u32[]{:S(2)}, u32[]{:S(2)}) collective-permute-start(f32[1,128]{1,0:T(1,128)S(1)} %fusion.after), channel_id=1, source_target_pairs={{0,64},{16,80},{32,96},{48,112},{64,0},{80,16},{96,32},{112,48},{1... | collective-permute-start | bytes 1544 | tf_op jit(solution)/shard_map/ppermute | solution.py:266
  16.0 0.9 %copy-start.3 = (f32[24,1024]{1,0:T(8,128)S(1)}, f32[24,1024]{1,0:T(8,128)}, u32[]{:S(2)}) copy-start(f32[24,1024]{1,0:T(8,128)} %get-tuple-element.15.around) | copy-start | bytes 294916
  17.0 11.9 %collective-permute-start.6 = (f32[16,1152]{1,0:T(8,128)S(1)}, f32[16,1152]{1,0:T(8,128)S(1)}, u32[]{:S(2)}, u32[]{:S(2)}) collective-permute-start(f32[16,1152]{1,0:T(8,128)S(1)} %get-tuple-element.22), channel_id=1, source_target_pairs={{16,32},{32,16},{17,33},{33,17},{18,34},{34,18},{19,35},{35,19},{4... | collective-permute-start | bytes 221192 | tf_op jit(solution)/shard_map/ppermute | solution.py:295
  19.7 3.6 %collective-permute-start.4 = (f32[1,128]{1,0:T(1,128)S(1)}, f32[1,128]{1,0:T(1,128)S(1)}, u32[]{:S(2)}, u32[]{:S(2)}) collective-permute-start(f32[1,128]{1,0:T(1,128)S(1)} %fusion.1.one), channel_id=1, source_target_pairs={{0,32},{16,48},{32,0},{48,16},{64,96},{80,112},{96,64},{112,80},{1... | collective-permute-start | bytes 1544 | tf_op jit(solution)/shard_map/ppermute | solution.py:266
  23.4 5.5 %collective-permute-start.5 = (f32[8,1152]{1,0:T(8,128)S(1)}, f32[8,1152]{1,0:T(8,128)S(1)}, u32[]{:S(2)}, u32[]{:S(2)}) collective-permute-start(f32[8,1152]{1,0:T(8,128)S(1)} %shard_map.84), channel_id=1, source_target_pairs={{0,16},{16,0},{32,48},{48,32},{64,80},{80,64},{96,112},{112,96},{1... | collective-permute-start | bytes 110600 | tf_op jit(solution)/shard_map/ppermute | solution.py:303

commit v3 on v2

--- a/solution.py
+++ b/solution.py
@@ -38,94 +38,114 @@
     return coriolis_sq, zonal_coef, east_coef
 
 
-def near_depth(depth_at, block, depth_rows, columns):
-    last = depth_rows // ROWS - 1
-    rows = [jnp.maximum(block - 1, 0), block, jnp.minimum(block + 1, last)]
-    return [depth_at[pl.ds(pl.multiple_of(r * ROWS, ROWS), ROWS), columns] for r in rows]
-
-
-def edges_kernel(height, east, north, depth, to_right, to_left, around, sems):
+def at_top():
+    return jnp.logical_and(lax.axis_index("lat") == 0, lax.axis_index("pole") == 0)
+
+
+def at_bottom():
+    last_band = lax.axis_index("lat") == lax.axis_size("lat") - 1
+    return jnp.logical_and(last_band, lax.axis_index("pole") == lax.axis_size("pole") - 1)
+
+
+def terms_near(blocks):
+    n_pole = lax.axis_size("pole")
+    first = (lax.axis_index("lat") * n_pole + lax.axis_index("pole") - blocks) * ROWS
+    index = first + lax.broadcasted_iota(jnp.int32, ((2 * blocks + 1) * ROWS, LANES), 0)
+    return row_terms(index.astype(F32), lax.axis_size("lat") * n_pole * ROWS)
+
+
+def own_field(high, eastward, northward, coef):
+    column = lax.broadcasted_iota(jnp.int32, (ROWS, COLS), 1)
+    row = lax.broadcasted_iota(jnp.int32, (ROWS, COLS), 0)
+    lane = lax.broadcasted_iota(jnp.int32, (ROWS, LANES), 1)
+    coef = jnp.concatenate([coef] * (COLS // LANES), axis=1)
+    after = jnp.where(column == COLS - 1, 0.0, pltpu.roll(eastward, COLS - 1, 1))
+    before = jnp.where(column == 0, 0.0, pltpu.roll(eastward, 1, 1))
+    below = jnp.where(row == ROWS - 1, 0.0, pltpu.roll(northward, ROWS - 1, 0))
+    above = jnp.where(row == 0, 0.0, pltpu.roll(northward, 1, 0))
+    partial = high - coef * (after - before) - north_scale * (below - above)
+    outer = jnp.where(lane < LANES // 2, eastward[:, 0:LANES], eastward[:, COLS - LANES :])
+    nothing = jnp.zeros((ROWS, LANES), F32)
+    return jnp.concatenate([partial, outer], axis=1), jnp.concatenate([northward, nothing], axis=1)
+
+
+def rows_kernel(height, east, north, depth, send_near, send_far, fields, sems):
     block = lax.axis_index("pole")
-    copies = []
-    for out, first in ((to_right, COLS - LANES), (to_left, 0)):
-        columns = pl.ds(first, LANES)
-        parts = [height.at[:, columns], east.at[:, columns], north.at[:, columns]]
-        parts += near_depth(depth.at, block, depth.shape[0], columns)
-        copies += [(part, out.at[pl.ds(i * ROWS, ROWS), :]) for i, part in enumerate(parts)]
-    parts = near_depth(depth.at, block, depth.shape[0], pl.ds(0, COLS))
-    copies += [(part, around.at[pl.ds(i * ROWS, ROWS), :]) for i, part in enumerate(parts)]
-    copies = [pltpu.make_async_copy(source, target, sems.at[i]) for i, (source, target) in enumerate(copies)]
+    own = pl.ds(pl.multiple_of(block * ROWS, ROWS), ROWS)
+    copies = [pltpu.make_async_copy(source, fields.at[i], sems.at[i]) for i, source in enumerate((height, east, north))]
+    copies.append(pltpu.make_async_copy(depth.at[own, :], fields.at[3], sems.at[3]))
     for copy in copies:
         copy.start()
+    unused, also_unused, coef = terms_near(0)
     for copy in copies:
         copy.wait()
-
-
-def near_kernel(rows, one, two, after, out):
-    out[0 : ROWS - 1, :] = rows[0 : ROWS - 1, :]
-    out[ROWS - 1 : ROWS, 0:LANES] = one[...] + two[...]
-    out[ROWS - 1 : ROWS, LANES:] = rows[ROWS - 1 : ROWS, LANES:]
-
-
-def rows_kernel(height, east, north, around, from_left, from_right, after, field, winds, depths, send_near, send_far, coriolis, zonal):
-    block, band = lax.axis_index("pole"), lax.axis_index("lat")
-    total_rows = lax.axis_size("lat") * lax.axis_size("pole") * ROWS
-    first_row = (band * lax.axis_size("pole") + block) * ROWS - ROWS
-    index = (first_row + lax.broadcasted_iota(jnp.int32, (3 * ROWS, LANES), 0)).astype(F32)
-    coriolis[...], zonal[...], east_coef = row_terms(index, total_rows)
-    east_coef = east_coef[ROWS : 2 * ROWS, :]
     even = lax.rem(block, 2) == 0
-    lane = lax.broadcasted_iota(jnp.int32, (ROWS, LANES), 1)
     row = lax.broadcasted_iota(jnp.int32, (ROWS, WIDE), 0)
-
-    def widened(own, part):
-        at = slice(part * ROWS, (part + 1) * ROWS)
-        return jnp.concatenate([own, jnp.where(lane < LANES // 2, from_right[at, :], from_left[at, :])], axis=1)
-
-    high = widened(height[...], 0)
-    eastward = widened(east[...], 1)
-    northward = widened(north[...], 2)
-    coef = jnp.concatenate([east_coef] * TILES, axis=1)
-    partial = high - coef * (pltpu.roll(eastward, WIDE - 1, 1) - pltpu.roll(eastward, 1, 1))
-    below = jnp.where(row == ROWS - 1, 0.0, pltpu.roll(northward, ROWS - 1, 0))
-    above = jnp.where(row == 0, 0.0, pltpu.roll(northward, 1, 0))
-    partial = partial - north_scale * (below - above)
-    field[...] = partial
-    winds[...] = northward
+    partial, northward = own_field(fields[0], fields[1], fields[2], coef)
     upward = jnp.where(row < HALO, partial, pltpu.roll(northward, HALO, 0))
     downward = jnp.where(row < HALO, pltpu.roll(partial, ROWS - 2, 0), pltpu.roll(northward, ROWS - 1, 0))
     send_near[...] = jnp.where(even, downward, upward)
     send_far[0:ROWS, :] = jnp.where(even, upward, downward)
-    for i in range(3):
-        part = widened(around[i * ROWS : (i + 1) * ROWS, :], 3 + i)
-        depths[i * ROWS : (i + 1) * ROWS, :] = part
-        if i == 1:
-            send_far[ROWS : 2 * ROWS, :] = part
-
-
-def solve_kernel(field, winds, depths, near, far, one, two, coriolis, zonal, out, rhs_w, depth_w, base_w, poles, gain, even_p, odd_p, result):
+    send_far[ROWS : 2 * ROWS, 0:COLS] = fields[3]
+    send_far[ROWS : 2 * ROWS, COLS:] = jnp.zeros((ROWS, LANES), F32)
+
+
+def columns_kernel(height, east, north, depth, near, far, field, depths, coriolis, zonal, east_coef, to_right, to_left):
     block = lax.axis_index("pole")
-    band = lax.axis_index("lat")
     even = lax.rem(block, 2) == 0
-    top = jnp.logical_and(band == 0, block == 0)
-    last_block = lax.axis_size("pole") - 1
-    bottom = jnp.logical_and(band == lax.axis_size("lat") - 1, block == last_block)
+    top, bottom, last_block = at_top(), at_bottom(), lax.axis_size("pole") - 1
+    coriolis[...], zonal[...], coef = terms_near(1)
+    east_coef[...] = coef
     row = lax.broadcasted_iota(jnp.int32, (ROWS, WIDE), 0)
-
-    near_rows, far_rows, far_depth = near[...], far[0:ROWS, :], far[ROWS : 2 * ROWS, :]
+    lane = lax.broadcasted_iota(jnp.int32, (ROWS, LANES), 1)
+    partial, northward = own_field(height[...], east[...], north[...], coef[ROWS : 2 * ROWS, :])
+
+    near_rows, far_rows, far_depth = near[...], far[0:ROWS, :], far[ROWS : 2 * ROWS, 0:COLS]
     upper = jnp.where(top, 0.0, jnp.where(even, far_rows, near_rows))
     lower = jnp.where(bottom, 0.0, jnp.where(even, near_rows, far_rows))
-    north = winds[...]
     from_above = north_scale * pltpu.roll(upper, ROWS - HALO, 0)
     from_below = north_scale * pltpu.roll(lower, 1, 0)
-    mid = field[...] + jnp.where(row == 0, from_above, 0.0) - jnp.where(row == ROWS - 1, from_below, 0.0)
-    own_first = jnp.where(top, 0.0, north_scale * pltpu.roll(north, ROWS - 1, 0))
-    own_last = jnp.where(bottom, 0.0, north_scale * pltpu.roll(north, 1, 0))
+    mid = partial + jnp.where(row == 0, from_above, 0.0) - jnp.where(row == ROWS - 1, from_below, 0.0)
+    own_first = jnp.where(top, 0.0, north_scale * pltpu.roll(northward, ROWS - 1, 0))
+    own_last = jnp.where(bottom, 0.0, north_scale * pltpu.roll(northward, 1, 0))
     above = pltpu.roll(upper, ROWS - HALO, 0) - jnp.where(row == ROWS - 1, own_first, 0.0)
     below = lower + jnp.where(row == 0, own_last, 0.0)
-    d_above = jnp.where(block == 0, far_depth, depths[0:ROWS, :])
-    d_mid = depths[ROWS : 2 * ROWS, :]
-    d_below = jnp.where(block == last_block, far_depth, depths[2 * ROWS : 3 * ROWS, :])
+    rows = [jnp.maximum(block - 1, 0), block, jnp.minimum(block + 1, last_block)]
+    deep = [depth[pl.ds(pl.multiple_of(r * ROWS, ROWS), ROWS), :] for r in rows]
+    deep[0] = jnp.where(block == 0, far_depth, deep[0])
+    deep[2] = jnp.where(block == last_block, far_depth, deep[2])
+    for i, (value, d) in enumerate(zip((above, mid, below), deep)):
+        at, later = slice(i * ROWS, (i + 1) * ROWS), slice((3 + i) * ROWS, (4 + i) * ROWS)
+        field[at, :] = value
+        depths[at, :] = d
+        winds = value[:, COLS:]
+        to_right[at, :] = jnp.where(lane == 0, pltpu.roll(winds, 1, 1), value[:, COLS - LANES : COLS])
+        to_left[at, :] = jnp.where(lane == LANES - 1, pltpu.roll(winds, LANES - 1, 1), value[:, 0:LANES])
+        to_right[later, :] = d[:, COLS - LANES :]
+        to_left[later, :] = d[:, 0:LANES]
+
+
+def merge_kernel(one, two, after, out):
+    out[...] = one[...] + two[...]
+
+
+def solve_kernel(field, depths, from_left, from_right, one, two, coriolis, zonal, east, out, rhs_w, depth_w, base_w, poles, gain, even_p, odd_p, result):
+    top, bottom = at_top(), at_bottom()
+    tile_lane = lax.broadcasted_iota(jnp.int32, (ROWS, LANES), 1)
+
+    def block_rows(i):
+        at, deep = slice(i * ROWS, (i + 1) * ROWS), slice((3 + i) * ROWS, (4 + i) * ROWS)
+        coef, winds = east[at, :], field[at, COLS:]
+        begin = field[at, 0:LANES] + jnp.where(tile_lane == 0, coef * from_left[at, :], 0.0)
+        end = field[at, COLS - LANES : COLS] - jnp.where(tile_lane == LANES - 1, coef * from_right[at, :], 0.0)
+        beyond = jnp.where(tile_lane < LANES // 2, from_right[at, :], from_left[at, :])
+        beyond = beyond + jnp.where(tile_lane == 0, coef * pltpu.roll(winds, 1, 1), 0.0)
+        beyond = beyond - jnp.where(tile_lane == LANES - 1, coef * pltpu.roll(winds, LANES - 1, 1), 0.0)
+        rhs = jnp.concatenate([begin, field[at, LANES : COLS - LANES], end, beyond], axis=1)
+        beyond = jnp.where(tile_lane < LANES // 2, from_right[deep, :], from_left[deep, :])
+        return rhs, jnp.concatenate([depths[at, :], beyond], axis=1)
+
+    parts = [block_rows(i) for i in range(3)]
 
     lane = lax.broadcasted_iota(jnp.int32, (ROWS, LANES), 1)
     sub = lax.broadcasted_iota(jnp.int32, (ROWS, LANES), 0)
@@ -139,7 +159,7 @@
             value = jnp.where(owner(q) == t, wide[:, q * LANES : (q + 1) * LANES], value)
         return jnp.take_along_axis(value, lax.rem(lane * TILES + t, LANES), axis=1)
 
-    for i, (rhs, deep) in enumerate(((above, d_above), (mid, d_mid), (below, d_below))):
+    for i, (rhs, deep) in enumerate(parts):
         at = slice(i * ROWS, (i + 1) * ROWS)
         z = zonal[at, :]
         for t in range(TILES):
@@ -152,7 +172,7 @@
                 d = jnp.where(bottom, 0.0, d)
             depth_w[t, at, :] = d
 
-    numbers = jnp.broadcast_to((one[...] + two[...]) + near[ROWS - 1 : ROWS, 0:LANES], (ROWS, LANES))
+    numbers = jnp.broadcast_to(one[...] + two[...], (ROWS, LANES))
     groups = POLES // ROWS
     for g in range(groups):
         for which in range(4):
@@ -254,6 +274,7 @@
 
 def body(height, east_wind, north_wind, depth, pole_real, pole_imag, weight_real, weight_imag):
     n_pole, n_lat, n_lon = (lax.axis_size(a) for a in ("pole", "lat", "lon"))
+
     pole = lax.axis_index("pole")
     at = lax.broadcasted_iota(jnp.int32, (1, LANES), 1)
     table = jnp.zeros((1, LANES), F32)
@@ -265,42 +286,44 @@
         pairs = [(2 * z + x, 2 * partner(z) + x) for z in range(layers) for x in range(2)]
         return lax.ppermute(table, "pole", pairs)
 
-    table = first = (table + swapped(table, lambda z: layers - 1 - z))[0:1]
-    table = table + swapped(table, lambda z: z ^ 2)
-    third = swapped(table, lambda z: z ^ 1)
-
-    column = shape(6 * ROWS, LANES)
-    to_right, to_left, around = pl.pallas_call(
-        edges_kernel,
-        out_shape=[column, column, shape(3 * ROWS, COLS)],
+    one = table + swapped(table, lambda z: layers - 1 - z)
+    two = swapped(one, lambda z: z ^ 2)
+
+    wide, both = shape(ROWS, WIDE), shape(2 * ROWS, WIDE)
+    send_near, send_far = pl.pallas_call(
+        rows_kernel,
+        out_shape=[wide, both],
         in_specs=[pl.BlockSpec(memory_space=pl.ANY)] * 4,
-        out_specs=[VMEM] * 3,
-        scratch_shapes=[pltpu.SemaphoreType.DMA((15,))],
+        out_specs=[VMEM] * 2,
+        scratch_shapes=[pltpu.VMEM((4, ROWS, COLS), F32), pltpu.SemaphoreType.DMA((4,))],
         compiler_params=pltpu.CompilerParams(vmem_limit_bytes=66600000),
     )(height, east_wind, north_wind, depth)
-    from_left = lax.ppermute(to_right, "lon", [(i, (i + 1) % n_lon) for i in range(n_lon)])
-    from_right = lax.ppermute(to_left, "lon", [((i + 1) % n_lon, i) for i in range(n_lon)])
-    wide, both = shape(ROWS, WIDE), shape(2 * ROWS, WIDE)
-    terms = shape(3 * ROWS, LANES)
-    field, winds, depths, send_near, send_far, coriolis, zonal = call(
-        rows_kernel, [wide, wide, shape(3 * ROWS, WIDE), wide, both, terms, terms], 7, 100000
-    )(height, east_wind, north_wind, around, from_left, from_right, first)
-
     total = n_lat * n_pole
     far_pairs = []
     for r in range(1, total, 2):
         for c in range(n_lon):
-            one, two = (((b % n_pole) * n_lat + b // n_pole) * n_lon + c for b in (r, (r + 1) % total))
-            far_pairs += [(one, two), (two, one)]
+            here, there = (((b % n_pole) * n_lat + b // n_pole) * n_lon + c for b in (r, (r + 1) % total))
+            far_pairs += [(here, there), (there, here)]
     far = lax.ppermute(send_far, ("pole", "lat", "lon"), far_pairs)
-    (send_near,) = pl.pallas_call(
-        near_kernel,
-        out_shape=[wide],
-        in_specs=[VMEM, VMEM, VMEM, pl.BlockSpec(memory_space=pl.ANY)],
+    beside = [(i, i ^ 1) for i in range(n_pole)]
+    near = lax.ppermute(send_near, "pole", beside)
+
+    tall, terms, column = shape(3 * ROWS, COLS), shape(3 * ROWS, LANES), shape(6 * ROWS, LANES)
+    field, depths, coriolis, zonal, east_coef, to_right, to_left = call(
+        columns_kernel, [shape(3 * ROWS, WIDE), tall, terms, terms, terms, column, column], 6, 100000
+    )(height, east_wind, north_wind, depth, near, far)
+    from_left = lax.ppermute(to_right, "lon", [(i, (i + 1) % n_lon) for i in range(n_lon)])
+    from_right = lax.ppermute(to_left, "lon", [((i + 1) % n_lon, i) for i in range(n_lon)])
+
+    (one,) = pl.pallas_call(
+        merge_kernel,
+        out_shape=[shape(1, LANES)],
+        in_specs=[VMEM, VMEM, pl.BlockSpec(memory_space=pl.ANY)],
         out_specs=[VMEM],
         compiler_params=pltpu.CompilerParams(vmem_limit_bytes=LIMIT),
-    )(send_near, table, third, first)
-    near = lax.ppermute(send_near, "pole", [(i, i ^ 1) for i in range(n_pole)])
+    )(one, two, to_right)
+    one = one + swapped(one, lambda z: z ^ 1)
+    two = lax.ppermute(one, "pole", beside)
 
     groups = POLES // ROWS
     tiles = pltpu.VMEM((TILES, 3 * ROWS, LANES), F32)
@@ -316,7 +339,7 @@
         pltpu.VMEM((groups, TILES, ROWS, LANES), F32),
     ]
     (out,) = call(solve_kernel, [shape(ROWS, COLS)], 9, 60000000, scratch)(
-        field, winds, depths, near, far, table, third, coriolis, zonal
+        field, depths, from_left, from_right, one, two, coriolis, zonal, east_coef
     )
     return out
 

time: 35.8 us -> 38.4 us (1.073); the launches traced: 35.1 us -> 38.1 us
  starting transfers between devices: 14.1 us -> 17.3 us
    ppermute x1 -> x2, starting transfers between devices: 1.41 us -> 6.15 us  [the longest x1 3.11 us: body(): near = lax.ppermute(send_near, 'pole', beside)]
    ppermute x3, waiting for transfers between devices: 3.53 us -> 7.14 us  [swapped(): return lax.ppermute(table, 'pole', pairs)]
    ppermute x1 -> x2, waiting for transfers between devices: 4.05 us -> 2.01 us  [the longest x1 2.01 us: body(): two = lax.ppermute(one, 'pole', beside)]
    ppermute x1, waiting for transfers between devices: 1.36 us -> 0.01 us  [body(): lax.ppermute(to_right, 'lon', [(i, (i + 1) % n_lon) for i in range(n_lon)])]
    ppermute x1, starting transfers between devices: 2.76 us -> 1.79 us  [body(): far = lax.ppermute(send_far, ('pole', 'lat', 'lon'), far_pairs)]
    ppermute x3, starting transfers between devices: 6.66 us -> 6.02 us  [swapped(): return lax.ppermute(table, 'pole', pairs)]
  transfers between devices with their start and end apart: 7 -> 8, of which waited for: 4 -> 3; matrix products, arithmetic and copies ran while one was open for 0% -> 0% of each run, Pallas kernels for 5% -> 0%
where the time goes in v3:
time: 38.4 us; the launch traced here: 38.1 us
  starting transfers between devices  17.3 us (45%)
  waiting for transfers between devices  9.16 us (24%)
  Pallas kernels  7.97 us (21%)
  between operations  2.67 us (7%)
  local copies, waits for them, and re-layouts  1.05 us (3%)
    ppermute x3, waiting for transfers between devices, swapped(): return lax.ppermute(table, 'pole', pairs)  7.14 us
    pallas_call x1, Pallas kernels, body(): call(solve_kernel, [shape(ROWS, COLS)], 9, 60000000, scratch)  6.26 us
    ppermute x3, starting transfers between devices, swapped(): return lax.ppermute(table, 'pole', pairs)  6.02 us
    ppermute x1, starting transfers between devices, body(): near = lax.ppermute(send_near, 'pole', beside)  3.11 us
    ppermute x1, starting transfers between devices, body(): two = lax.ppermute(one, 'pole', beside)  3.03 us
    ppermute x1, waiting for transfers between devices, body(): two = lax.ppermute(one, 'pole', beside)  2.01 us
    ppermute x1, starting transfers between devices, body(): far = lax.ppermute(send_far, ('pole', 'lat', 'lon'), far_pairs)  1.79 us
    ppermute x1, starting transfers between devices, body(): lax.ppermute(to_left, 'lon', [((i + 1) % n_lon, i) for i in range(n_lon)])  1.66 us
  transfers between devices with their start and end apart: 8, of which 3 were waited for; matrix products, arithmetic and copies ran while one was open for 0% of the time, Pallas kernels for 0%

profile of v3, /device:TPU:32, one launch (start us, length us, event | category | flops | bytes accessed | tf_op | source)
XLA Modules:
  0.0 38.1 jit_solution(8441718225744448415)
XLA Ops:
  0.0 1.6 %shard_map.82 = (f32[8,1152]{1,0:T(8,128)}, f32[16,1152]{1,0:T(8,128)}) custom-call(f32[8,1024]{1,0:T(8,128)} %height.3, f32[8,1024]{1,0:T(8,128)} %east.3, f32[8,1024]{1,0:T(8,128)} %north.3, f32[128,1024]{1,0:T(8,128)} %depth.3), custom_call_target="tpu_custom_call" | custom-call | tf_op jit(solution)/shard_map/pallas_call | solution.py:293
  1.6 0.0 copy-start.1
  1.6 3.1 %collective-permute-start = (f32[8,1152]{1,0:T(8,128)}, f32[8,1152]{1,0:T(8,128)S(1)}, u32[]{:S(2)}, u32[]{:S(2)}) collective-permute-start(f32[8,1152]{1,0:T(8,128)} %get-tuple-element.14), channel_id=1, source_target_pairs={{0,16},{16,0},{32,48},{48,32},{64,80},{80,64},{96,112},{112,96},{1... | collective-permute-start | bytes 110600 | tf_op jit(solution)/shard_map/ppermute | solution.py:309
  4.7 1.8 %collective-permute-start.1 = (f32[16,1152]{1,0:T(8,128)}, f32[16,1152]{1,0:T(8,128)S(1)}, u32[]{:S(2)}, u32[]{:S(2)}) collective-permute-start(f32[16,1152]{1,0:T(8,128)} %get-tuple-element.15), channel_id=1, source_target_pairs={{16,32},{32,16},{17,33},{33,17},{18,34},{34,18},{19,35},{35,19},{4... | collective-permute-start | bytes 221192 | tf_op jit(solution)/shard_map/ppermute | solution.py:307
  9.1 5.1 %collective-permute-start.4 = (f32[1,128]{1,0:T(1,128)S(1)}, f32[1,128]{1,0:T(1,128)S(1)}, u32[]{:S(2)}, u32[]{:S(2)}) collective-permute-start(f32[1,128]{1,0:T(1,128)S(1)} %compare_select_fusion.3), channel_id=1, source_target_pairs={{0,224},{16,240},{32,192},{48,208},{64,160},{80,176},{96,128},{112... | collective-permute-start | bytes 1544 | tf_op jit(solution)/shard_map/ppermute | solution.py:287
  14.2 0.0 collective-permute-done.near
  14.2 0.0 collective-permute-done.1.far
  14.2 0.0 copy-done.2
  14.2 0.0 copy-done.3
  14.3 0.0 copy-start
  14.3 1.0 %copy-done = f32[128,1024]{1,0:T(8,128)S(1)} copy-done((f32[128,1024]{1,0:T(8,128)S(1)}, f32[128,1024]{1,0:T(8,128)}, u32[]{:S(2)}) %copy-start) | copy-done | bytes 524312
  15.3 0.1 shard_map.83
  15.4 1.7 %collective-permute-start.2 = (f32[48,128]{1,0:T(8,128)S(1)}, f32[48,128]{1,0:T(8,128)S(1)}, u32[]{:S(2)}, u32[]{:S(2)}) collective-permute-start(f32[48,128]{1,0:T(8,128)S(1)} %get-tuple-element.18.after), channel_id=1, source_target_pairs={{0,1},{1,2},{2,3},{3,0},{4,5},{5,6},{6,7},{7,4},{8,9},{9,10},{10,1... | collective-permute-start | bytes 73736 | tf_op jit(solution)/shard_map/ppermute | solution.py:315
  17.1 1.7 %collective-permute-start.3 = (f32[48,128]{1,0:T(8,128)S(1)}, f32[48,128]{1,0:T(8,128)S(1)}, u32[]{:S(2)}, u32[]{:S(2)}) collective-permute-start(f32[48,128]{1,0:T(8,128)S(1)} %get-tuple-element.19), channel_id=1, source_target_pairs={{1,0},{2,1},{3,2},{0,3},{5,4},{6,5},{7,6},{4,7},{9,8},{10,9},{11,1... | collective-permute-start | bytes 73736 | tf_op jit(solution)/shard_map/ppermute | solution.py:316
  18.7 0.0 collective-permute-done.4
  18.8 0.8 %collective-permute-start.5 = (f32[1,128]{1,0:T(1,128)S(1)}, f32[1,128]{1,0:T(1,128)S(1)}, u32[]{:S(2)}, u32[]{:S(2)}) collective-permute-start(f32[1,128]{1,0:T(1,128)S(1)} %fusion.one), channel_id=1, source_target_pairs={{0,64},{16,80},{32,96},{48,112},{64,0},{80,16},{96,32},{112,48},{1... | collective-permute-start | bytes 1544 | tf_op jit(solution)/shard_map/ppermute | solution.py:287
  19.6 3.7 %collective-permute-done.5.two = f32[1,128]{1,0:T(1,128)S(1)} collective-permute-done((f32[1,128]{1,0:T(1,128)S(1)}, f32[1,128]{1,0:T(1,128)S(1)}, u32[]{:S(2)}, u32[]{:S(2)}) %collective-permute-start.5) | collective-permute-done | bytes 544 | tf_op jit(solution)/shard_map/ppermute | solution.py:287
  23.3 0.1 collective-permute-start.6
  23.4 3.4 %collective-permute-done.6 = f32[1,128]{1,0:T(1,128)S(1)} collective-permute-done((f32[1,128]{1,0:T(1,128)S(1)}, f32[1,128]{1,0:T(1,128)S(1)}, u32[]{:S(2)}, u32[]{:S(2)}) %collective-permute-start.6) | collective-permute-done | bytes 544 | tf_op jit(solution)/shard_map/ppermute | solution.py:287
  26.8 3.0 %collective-permute-start.7 = (f32[1,128]{1,0:T(1,128)S(1)}, f32[1,128]{1,0:T(1,128)S(1)}, u32[]{:S(2)}, u32[]{:S(2)}) collective-permute-start(f32[1,128]{1,0:T(1,128)S(1)} %add.7.one), channel_id=1, source_target_pairs={{0,16},{16,0},{32,48},{48,32},{64,80},{80,64},{96,112},{112,96},{1... | collective-permute-start | bytes 1544 | tf_op jit(solution)/shard_map/ppermute | solution.py:326
  29.9 2.0 %collective-permute-done.7.two = f32[1,128]{1,0:T(1,128)S(1)} collective-permute-done((f32[1,128]{1,0:T(1,128)S(1)}, f32[1,128]{1,0:T(1,128)S(1)}, u32[]{:S(2)}, u32[]{:S(2)}) %collective-permute-start.7) | collective-permute-done | bytes 544 | tf_op jit(solution)/shard_map/ppermute | solution.py:326
  31.9 0.0 collective-permute-done.2.from_left
  31.9 0.0 collective-permute-done.3.from_right
  31.9 6.3 %shard_map.85 = f32[8,1024]{1,0:T(8,128)} custom-call(f32[24,1152]{1,0:T(8,128)S(1)} %get-tuple-element.16.field, f32[24,1024]{1,0:T(8,128)S(1)} %get-tuple-element.17.depths, f32[48,128]{1,0:T(8,128)S(1)} %collective-permute-done.2.from_left, f32[48,128]{1,0:T(8,128)S(1)} %collective-permute-done.3.from_right, f32[1,128]{1,0:T(1,128)S(1)} %add.7.one, ...), custom_call_target="tpu_custom_call" | custom-call | flops 60000000 | bytes 200000 | tf_op jit(solution)/shard_map/pallas_call | solution.py:341
  (7 shorter events, 0.0 us)
Async XLA Ops:
  0.0 14.2 %copy-start.2 = (f32[8,1024]{1,0:T(8,128)S(1)}, f32[8,1024]{1,0:T(8,128)}, u32[]{:S(2)}) copy-start(f32[8,1024]{1,0:T(8,128)} %east.3) | copy-start | bytes 98308
  0.0 14.2 %copy-start.3 = (f32[8,1024]{1,0:T(8,128)S(1)}, f32[8,1024]{1,0:T(8,128)}, u32[]{:S(2)}) copy-start(f32[8,1024]{1,0:T(8,128)} %north.3) | copy-start | bytes 98308
  1.6 12.6 %copy-start.1 = (f32[8,1024]{1,0:T(8,128)S(1)}, f32[8,1024]{1,0:T(8,128)}, u32[]{:S(2)}) copy-start(f32[8,1024]{1,0:T(8,128)} %height.3) | copy-start | bytes 98308
  1.6 12.6 %collective-permute-start = (f32[8,1152]{1,0:T(8,128)}, f32[8,1152]{1,0:T(8,128)S(1)}, u32[]{:S(2)}, u32[]{:S(2)}) collective-permute-start(f32[8,1152]{1,0:T(8,128)} %get-tuple-element.14), channel_id=1, source_target_pairs={{0,16},{16,0},{32,48},{48,32},{64,80},{80,64},{96,112},{112,96},{1... | collective-permute-start | bytes 110600 | tf_op jit(solution)/shard_map/ppermute | solution.py:309
  4.7 9.5 %collective-permute-start.1 = (f32[16,1152]{1,0:T(8,128)}, f32[16,1152]{1,0:T(8,128)S(1)}, u32[]{:S(2)}, u32[]{:S(2)}) collective-permute-start(f32[16,1152]{1,0:T(8,128)} %get-tuple-element.15), channel_id=1, source_target_pairs={{16,32},{32,16},{17,33},{33,17},{18,34},{34,18},{19,35},{35,19},{4... | collective-permute-start | bytes 221192 | tf_op jit(solution)/shard_map/ppermute | solution.py:307
  9.1 9.6 %collective-permute-start.4 = (f32[1,128]{1,0:T(1,128)S(1)}, f32[1,128]{1,0:T(1,128)S(1)}, u32[]{:S(2)}, u32[]{:S(2)}) collective-permute-start(f32[1,128]{1,0:T(1,128)S(1)} %compare_select_fusion.3), channel_id=1, source_target_pairs={{0,224},{16,240},{32,192},{48,208},{64,160},{80,176},{96,128},{112... | collective-permute-start | bytes 1544 | tf_op jit(solution)/shard_map/ppermute | solution.py:287
  14.3 1.0 %copy-start = (f32[128,1024]{1,0:T(8,128)S(1)}, f32[128,1024]{1,0:T(8,128)}, u32[]{:S(2)}) copy-start(f32[128,1024]{1,0:T(8,128)} %depth.3) | copy-start | bytes 1572868
  15.4 16.5 %collective-permute-start.2 = (f32[48,128]{1,0:T(8,128)S(1)}, f32[48,128]{1,0:T(8,128)S(1)}, u32[]{:S(2)}, u32[]{:S(2)}) collective-permute-start(f32[48,128]{1,0:T(8,128)S(1)} %get-tuple-element.18.after), channel_id=1, source_target_pairs={{0,1},{1,2},{2,3},{3,0},{4,5},{5,6},{6,7},{7,4},{8,9},{9,10},{10,1... | collective-permute-start | bytes 73736 | tf_op jit(solution)/shard_map/ppermute | solution.py:315
  17.1 14.8 %collective-permute-start.3 = (f32[48,128]{1,0:T(8,128)S(1)}, f32[48,128]{1,0:T(8,128)S(1)}, u32[]{:S(2)}, u32[]{:S(2)}) collective-permute-start(f32[48,128]{1,0:T(8,128)S(1)} %get-tuple-element.19), channel_id=1, source_target_pairs={{1,0},{2,1},{3,2},{0,3},{5,4},{6,5},{7,6},{4,7},{9,8},{10,9},{11,1... | collective-permute-start | bytes 73736 | tf_op jit(solution)/shard_map/ppermute | solution.py:316
  18.8 4.5 %collective-permute-start.5 = (f32[1,128]{1,0:T(1,128)S(1)}, f32[1,128]{1,0:T(1,128)S(1)}, u32[]{:S(2)}, u32[]{:S(2)}) collective-permute-start(f32[1,128]{1,0:T(1,128)S(1)} %fusion.one), channel_id=1, source_target_pairs={{0,64},{16,80},{32,96},{48,112},{64,0},{80,16},{96,32},{112,48},{1... | collective-permute-start | bytes 1544 | tf_op jit(solution)/shard_map/ppermute | solution.py:287
  23.3 3.5 %collective-permute-start.6 = (f32[1,128]{1,0:T(1,128)S(1)}, f32[1,128]{1,0:T(1,128)S(1)}, u32[]{:S(2)}, u32[]{:S(2)}) collective-permute-start(f32[1,128]{1,0:T(1,128)S(1)} %shard_map.84), channel_id=1, source_target_pairs={{0,32},{16,48},{32,0},{48,16},{64,96},{80,112},{96,64},{112,80},{1... | collective-permute-start | bytes 1544 | tf_op jit(solution)/shard_map/ppermute | solution.py:287
  26.8 5.0 %collective-permute-start.7 = (f32[1,128]{1,0:T(1,128)S(1)}, f32[1,128]{1,0:T(1,128)S(1)}, u32[]{:S(2)}, u32[]{:S(2)}) collective-permute-start(f32[1,128]{1,0:T(1,128)S(1)} %add.7.one), channel_id=1, source_target_pairs={{0,16},{16,0},{32,48},{48,32},{64,80},{80,64},{96,112},{112,96},{1... | collective-permute-start | bytes 1544 | tf_op jit(solution)/shard_map/ppermute | solution.py:326

commit v4 on v2

--- a/solution.py
+++ b/solution.py
@@ -1,3 +1,4 @@
+import functools
 import math
 
 import jax
@@ -61,7 +62,7 @@
         copy.wait()
 
 
-def near_kernel(rows, one, two, after, out):
+def near_kernel(rows, one, two, out):
     out[0 : ROWS - 1, :] = rows[0 : ROWS - 1, :]
     out[ROWS - 1 : ROWS, 0:LANES] = one[...] + two[...]
     out[ROWS - 1 : ROWS, LANES:] = rows[ROWS - 1 : ROWS, LANES:]
@@ -186,6 +187,7 @@
         last = m == len(relax_weights) - 1
 
         def one_row(g, j):
+            weighted = []
             z = jnp.broadcast_to(zonal[pl.ds(j, 1), :], (ROWS, LANES))
             here = [[old[g, c, j, t] for t in range(TILES)] for c in range(2)]
             west = [pltpu.roll(here[c][TILES - 1], 1, 1) for c in range(2)]
@@ -204,31 +206,27 @@
                     u_real = u_real + ((1.0 - w) / w) * here[0][t]
                     u_imag = u_imag + ((1.0 - w) / w) * here[1][t]
                 if last:
-                    wreal, wimag = alpha * poles[g, 2], alpha * poles[g, 3]
-                    value = jnp.sum(wreal * u_real - wimag * u_imag, axis=0, keepdims=True)
-                    result[g, t, pl.ds(j - ROWS, 1), :] = value
+                    weighted.append(weights[g][0] * u_real - weights[g][1] * u_imag)
                 else:
                     new[g, 0, j, t] = u_real
                     new[g, 1, j, t] = u_imag
-
-        def sweep(i, carry):
-            for g in range(groups):
-                for k in range(2):
-                    one_row(g, low + 2 * i + k)
-            return carry
-
-        lax.fori_loop(0, (high - low) // 2, sweep, 0)
+            return weighted
+
+        if last:
+            weights = [[alpha * poles[g, which] for which in (2, 3)] for g in range(groups)]
+        for j in range(low, high):
+            weighted = [one_row(g, j) for g in range(groups)]
+            for t in range(TILES if last else 0):
+                value = functools.reduce(jnp.add, [of_group[t] for of_group in weighted])
+                result[t, j - ROWS : j - ROWS + 1, :] = jnp.sum(value, axis=0, keepdims=True)
         if w != 1.0:
             alpha = alpha * w
             rhs_w[...] = rhs_w[...] * (1.0 / w)
 
     undealt = []
     for t in range(TILES):
-        value = result[0, t]
-        for g in range(1, groups):
-            value = value + result[g, t]
         index = lax.rem((lane - t + LANES) * INVERSE, LANES)
-        undealt.append(jnp.take_along_axis(value, index, axis=1))
+        undealt.append(jnp.take_along_axis(result[t], index, axis=1))
     for q in range(COLS // LANES):
         value = undealt[0]
         for t in range(1, TILES):
@@ -296,10 +294,10 @@
     (send_near,) = pl.pallas_call(
         near_kernel,
         out_shape=[wide],
-        in_specs=[VMEM, VMEM, VMEM, pl.BlockSpec(memory_space=pl.ANY)],
+        in_specs=[VMEM, VMEM, VMEM],
         out_specs=[VMEM],
         compiler_params=pltpu.CompilerParams(vmem_limit_bytes=LIMIT),
-    )(send_near, table, third, first)
+    )(send_near, table, third)
     near = lax.ppermute(send_near, "pole", [(i, i ^ 1) for i in range(n_pole)])
 
     groups = POLES // ROWS
@@ -313,7 +311,7 @@
         pltpu.VMEM((groups, 2, 3 * ROWS, TILES, ROWS, LANES), F32),
         iterate,
         iterate,
-        pltpu.VMEM((groups, TILES, ROWS, LANES), F32),
+        pltpu.VMEM((TILES, ROWS, LANES), F32),
     ]
     (out,) = call(solve_kernel, [shape(ROWS, COLS)], 9, 60000000, scratch)(
         field, winds, depths, near, far, table, third, coriolis, zonal

time: 35.8 us -> 35.2 us (0.983)
  the two profiles are of different devices: /device:TPU:32 before, /device:TPU:8 now
where the time goes in v4:
time: 35.2 us; the launch traced here: 35 us
  starting transfers between devices  16.9 us (48%)
  Pallas kernels  7.46 us (21%)
  waiting for transfers between devices  7.09 us (20%)
  between operations  2.64 us (7%)
  local copies, waits for them, and re-layouts  0.9 us (3%)
    ppermute x3, starting transfers between devices, swapped(): return lax.ppermute(table, 'pole', pairs)  12.2 us
    pallas_call x1, Pallas kernels, body(): call(solve_kernel, [shape(ROWS, COLS)], 9, 60000000, scratch)  5.63 us
    ppermute x1, waiting for transfers between devices, body(): near = lax.ppermute(send_near, 'pole', [(i, i ^ 1) for i in range(n_pole)])  3.74 us
    ppermute x3, waiting for transfers between devices, swapped(): return lax.ppermute(table, 'pole', pairs)  2.21 us
    pallas_call x1, Pallas kernels, body(): pl.pallas_call(edges_kernel, out_shape=[column, column, shape(3 * ROWS, C...  1.73 us
    ppermute x1, starting transfers between devices, body(): near = lax.ppermute(send_near, 'pole', [(i, i ^ 1) for i in range(n_pole)])  1.72 us
    ppermute x1, starting transfers between devices, body(): lax.ppermute(to_right, 'lon', [(i, (i + 1) % n_lon) for i in range(n_lon)])  1.65 us
    ppermute x1, waiting for transfers between devices, body(): lax.ppermute(to_left, 'lon', [((i + 1) % n_lon, i) for i in range(n_lon)])  1.13 us
  transfers between devices with their start and end apart: 7, of which 3 were waited for; matrix products, arithmetic and copies ran while one was open for 0% of the time, Pallas kernels for 5%

profile of v4, /device:TPU:8, one launch (start us, length us, event | category | flops | bytes accessed | tf_op | source)
XLA Modules:
  0.0 35.0 jit_solution(5697311658403096157)
XLA Ops:
  2.6 5.9 %collective-permute-start.2 = (f32[1,128]{1,0:T(1,128)S(1)}, f32[1,128]{1,0:T(1,128)S(1)}, u32[]{:S(2)}, u32[]{:S(2)}) collective-permute-start(f32[1,128]{1,0:T(1,128)S(1)} %compare_select_fusion.3), channel_id=1, source_target_pairs={{0,224},{16,240},{32,192},{48,208},{64,160},{80,176},{96,128},{112... | collective-permute-start | bytes 1544 | tf_op jit(solution)/shard_map/ppermute | solution.py:264
  8.5 0.0 copy-start
  8.5 0.0 copy-start.1
  8.6 1.7 %shard_map.82 = (f32[48,128]{1,0:T(8,128)}, f32[48,128]{1,0:T(8,128)}, f32[24,1024]{1,0:T(8,128)}) custom-call(f32[8,1024]{1,0:T(8,128)} %height.3, f32[8,1024]{1,0:T(8,128)} %east.3, f32[8,1024]{1,0:T(8,128)} %north.3, f32[128,1024]{1,0:T(8,128)} %depth.1), custom_call_target="tpu_custom_call" | custom-call | tf_op jit(solution)/shard_map/pallas_call | solution.py:271
  10.3 1.7 %collective-permute-start = (f32[48,128]{1,0:T(8,128)}, f32[48,128]{1,0:T(8,128)S(1)}, u32[]{:S(2)}, u32[]{:S(2)}) collective-permute-start(f32[48,128]{1,0:T(8,128)} %get-tuple-element.16), channel_id=1, source_target_pairs={{0,1},{1,2},{2,3},{3,0},{4,5},{5,6},{6,7},{7,4},{8,9},{9,10},{10,1... | collective-permute-start | bytes 73736 | tf_op jit(solution)/shard_map/ppermute | solution.py:279
  11.9 0.4 %collective-permute-start.1 = (f32[48,128]{1,0:T(8,128)}, f32[48,128]{1,0:T(8,128)S(1)}, u32[]{:S(2)}, u32[]{:S(2)}) collective-permute-start(f32[48,128]{1,0:T(8,128)} %get-tuple-element.17), channel_id=1, source_target_pairs={{1,0},{2,1},{3,2},{0,3},{5,4},{6,5},{7,6},{4,7},{9,8},{10,9},{11,1... | collective-permute-start | bytes 73736 | tf_op jit(solution)/shard_map/ppermute | solution.py:280
  12.4 0.0 collective-permute-done.2
  12.4 2.4 %collective-permute-start.3 = (f32[1,128]{1,0:T(1,128)S(1)}, f32[1,128]{1,0:T(1,128)S(1)}, u32[]{:S(2)}, u32[]{:S(2)}) collective-permute-start(f32[1,128]{1,0:T(1,128)S(1)} %fusion.after), channel_id=1, source_target_pairs={{0,64},{16,80},{32,96},{48,112},{64,0},{80,16},{96,32},{112,48},{1... | collective-permute-start | bytes 1544 | tf_op jit(solution)/shard_map/ppermute | solution.py:264
  14.8 0.0 collective-permute-done.from_left
  14.8 1.1 %collective-permute-done.1.from_right = f32[48,128]{1,0:T(8,128)S(1)} collective-permute-done((f32[48,128]{1,0:T(8,128)}, f32[48,128]{1,0:T(8,128)S(1)}, u32[]{:S(2)}, u32[]{:S(2)}) %collective-permute-start.1) | collective-permute-done | bytes 24608 | tf_op jit(solution)/shard_map/ppermute | solution.py:280
  16.0 0.0 copy-done
  16.0 0.0 copy-done.1
  16.0 0.0 copy-done.2
  16.0 0.0 copy-start.3
  16.0 0.9 %copy-done.3 = f32[24,1024]{1,0:T(8,128)S(1)} copy-done((f32[24,1024]{1,0:T(8,128)S(1)}, f32[24,1024]{1,0:T(8,128)}, u32[]{:S(2)}) %copy-start.3) | copy-done | bytes 98328
  16.9 0.1 shard_map.83
  17.0 0.9 %collective-permute-start.6 = (f32[16,1152]{1,0:T(8,128)S(1)}, f32[16,1152]{1,0:T(8,128)S(1)}, u32[]{:S(2)}, u32[]{:S(2)}) collective-permute-start(f32[16,1152]{1,0:T(8,128)S(1)} %get-tuple-element.22), channel_id=1, source_target_pairs={{16,32},{32,16},{17,33},{33,17},{18,34},{34,18},{19,35},{35,19},{4... | collective-permute-start | bytes 221192 | tf_op jit(solution)/shard_map/ppermute | solution.py:293
  17.9 0.0 collective-permute-done.3
  17.9 3.8 %collective-permute-start.4 = (f32[1,128]{1,0:T(1,128)S(1)}, f32[1,128]{1,0:T(1,128)S(1)}, u32[]{:S(2)}, u32[]{:S(2)}) collective-permute-start(f32[1,128]{1,0:T(1,128)S(1)} %fusion.1.one), channel_id=1, source_target_pairs={{0,32},{16,48},{32,0},{48,16},{64,96},{80,112},{96,64},{112,80},{1... | collective-permute-start | bytes 1544 | tf_op jit(solution)/shard_map/ppermute | solution.py:264
  21.7 2.2 %collective-permute-done.4.two = f32[1,128]{1,0:T(1,128)S(1)} collective-permute-done((f32[1,128]{1,0:T(1,128)S(1)}, f32[1,128]{1,0:T(1,128)S(1)}, u32[]{:S(2)}, u32[]{:S(2)}) %collective-permute-start.4) | collective-permute-done | bytes 544 | tf_op jit(solution)/shard_map/ppermute | solution.py:264
  23.9 1.7 %collective-permute-start.5 = (f32[8,1152]{1,0:T(8,128)S(1)}, f32[8,1152]{1,0:T(8,128)S(1)}, u32[]{:S(2)}, u32[]{:S(2)}) collective-permute-start(f32[8,1152]{1,0:T(8,128)S(1)} %shard_map.84), channel_id=1, source_target_pairs={{0,16},{16,0},{32,48},{48,32},{64,80},{80,64},{96,112},{112,96},{1... | collective-permute-start | bytes 110600 | tf_op jit(solution)/shard_map/ppermute | solution.py:301
  25.6 3.7 %collective-permute-done.5.near = f32[8,1152]{1,0:T(8,128)S(1)} collective-permute-done((f32[8,1152]{1,0:T(8,128)S(1)}, f32[8,1152]{1,0:T(8,128)S(1)}, u32[]{:S(2)}, u32[]{:S(2)}) %collective-permute-start.5) | collective-permute-done | bytes 36896 | tf_op jit(solution)/shard_map/ppermute | solution.py:301
  29.3 0.0 collective-permute-done.6.far
  29.3 5.6 %shard_map.85 = f32[8,1024]{1,0:T(8,128)} custom-call(f32[8,1152]{1,0:T(8,128)S(1)} %get-tuple-element.18.field, f32[8,1152]{1,0:T(8,128)S(1)} %get-tuple-element.19.winds, f32[24,1152]{1,0:T(8,128)S(1)} %get-tuple-element.20.depths, f32[8,1152]{1,0:T(8,128)S(1)} %collective-permute-done.5.near, f32[16,1152]{1,0:T(8,128)S(1)} %collective-permute-done.6.far, ...), custom_call_target="tpu_custom_call" | custom-call | flops 60000000 | bytes 200000 | tf_op jit(solution)/shard_map/pallas_call | solution.py:316
  (5 shorter events, 0.0 us)
Async XLA Ops:
  2.6 9.8 %collective-permute-start.2 = (f32[1,128]{1,0:T(1,128)S(1)}, f32[1,128]{1,0:T(1,128)S(1)}, u32[]{:S(2)}, u32[]{:S(2)}) collective-permute-start(f32[1,128]{1,0:T(1,128)S(1)} %compare_select_fusion.3), channel_id=1, source_target_pairs={{0,224},{16,240},{32,192},{48,208},{64,160},{80,176},{96,128},{112... | collective-permute-start | bytes 1544 | tf_op jit(solution)/shard_map/ppermute | solution.py:264
  8.5 7.4 %copy-start = (f32[8,1024]{1,0:T(8,128)S(1)}, f32[8,1024]{1,0:T(8,128)}, u32[]{:S(2)}) copy-start(f32[8,1024]{1,0:T(8,128)} %height.3) | copy-start | bytes 98308
  8.5 7.4 %copy-start.1 = (f32[8,1024]{1,0:T(8,128)S(1)}, f32[8,1024]{1,0:T(8,128)}, u32[]{:S(2)}) copy-start(f32[8,1024]{1,0:T(8,128)} %east.3) | copy-start | bytes 98308
  8.6 7.4 %copy-start.2 = (f32[8,1024]{1,0:T(8,128)S(1)}, f32[8,1024]{1,0:T(8,128)}, u32[]{:S(2)}) copy-start(f32[8,1024]{1,0:T(8,128)} %north.3) | copy-start | bytes 98308
  10.3 4.6 %collective-permute-start = (f32[48,128]{1,0:T(8,128)}, f32[48,128]{1,0:T(8,128)S(1)}, u32[]{:S(2)}, u32[]{:S(2)}) collective-permute-start(f32[48,128]{1,0:T(8,128)} %get-tuple-element.16), channel_id=1, source_target_pairs={{0,1},{1,2},{2,3},{3,0},{4,5},{5,6},{6,7},{7,4},{8,9},{9,10},{10,1... | collective-permute-start | bytes 73736 | tf_op jit(solution)/shard_map/ppermute | solution.py:279
  11.9 4.0 %collective-permute-start.1 = (f32[48,128]{1,0:T(8,128)}, f32[48,128]{1,0:T(8,128)S(1)}, u32[]{:S(2)}, u32[]{:S(2)}) collective-permute-start(f32[48,128]{1,0:T(8,128)} %get-tuple-element.17), channel_id=1, source_target_pairs={{1,0},{2,1},{3,2},{0,3},{5,4},{6,5},{7,6},{4,7},{9,8},{10,9},{11,1... | collective-permute-start | bytes 73736 | tf_op jit(solution)/shard_map/ppermute | solution.py:280
  12.4 5.5 %collective-permute-start.3 = (f32[1,128]{1,0:T(1,128)S(1)}, f32[1,128]{1,0:T(1,128)S(1)}, u32[]{:S(2)}, u32[]{:S(2)}) collective-permute-start(f32[1,128]{1,0:T(1,128)S(1)} %fusion.after), channel_id=1, source_target_pairs={{0,64},{16,80},{32,96},{48,112},{64,0},{80,16},{96,32},{112,48},{1... | collective-permute-start | bytes 1544 | tf_op jit(solution)/shard_map/ppermute | solution.py:264
  16.0 0.9 %copy-start.3 = (f32[24,1024]{1,0:T(8,128)S(1)}, f32[24,1024]{1,0:T(8,128)}, u32[]{:S(2)}) copy-start(f32[24,1024]{1,0:T(8,128)} %get-tuple-element.15.around) | copy-start | bytes 294916
  17.0 12.4 %collective-permute-start.6 = (f32[16,1152]{1,0:T(8,128)S(1)}, f32[16,1152]{1,0:T(8,128)S(1)}, u32[]{:S(2)}, u32[]{:S(2)}) collective-permute-start(f32[16,1152]{1,0:T(8,128)S(1)} %get-tuple-element.22), channel_id=1, source_target_pairs={{16,32},{32,16},{17,33},{33,17},{18,34},{34,18},{19,35},{35,19},{4... | collective-permute-start | bytes 221192 | tf_op jit(solution)/shard_map/ppermute | solution.py:293
  17.9 6.0 %collective-permute-start.4 = (f32[1,128]{1,0:T(1,128)S(1)}, f32[1,128]{1,0:T(1,128)S(1)}, u32[]{:S(2)}, u32[]{:S(2)}) collective-permute-start(f32[1,128]{1,0:T(1,128)S(1)} %fusion.1.one), channel_id=1, source_target_pairs={{0,32},{16,48},{32,0},{48,16},{64,96},{80,112},{96,64},{112,80},{1... | collective-permute-start | bytes 1544 | tf_op jit(solution)/shard_map/ppermute | solution.py:264
  23.9 5.5 %collective-permute-start.5 = (f32[8,1152]{1,0:T(8,128)S(1)}, f32[8,1152]{1,0:T(8,128)S(1)}, u32[]{:S(2)}, u32[]{:S(2)}) collective-permute-start(f32[8,1152]{1,0:T(8,128)S(1)} %shard_map.84), channel_id=1, source_target_pairs={{0,16},{16,0},{32,48},{48,32},{64,80},{80,64},{96,112},{112,96},{1... | collective-permute-start | bytes 110600 | tf_op jit(solution)/shard_map/ppermute | solution.py:301

commit v5 on v4

--- a/solution.py
+++ b/solution.py
@@ -45,7 +45,7 @@
     return [depth_at[pl.ds(pl.multiple_of(r * ROWS, ROWS), ROWS), columns] for r in rows]
 
 
-def edges_kernel(height, east, north, depth, to_right, to_left, around, sems):
+def edges_kernel(height, east, north, depth, to_right, to_left, sems):
     block = lax.axis_index("pole")
     copies = []
     for out, first in ((to_right, COLS - LANES), (to_left, 0)):
@@ -53,8 +53,6 @@
         parts = [height.at[:, columns], east.at[:, columns], north.at[:, columns]]
         parts += near_depth(depth.at, block, depth.shape[0], columns)
         copies += [(part, out.at[pl.ds(i * ROWS, ROWS), :]) for i, part in enumerate(parts)]
-    parts = near_depth(depth.at, block, depth.shape[0], pl.ds(0, COLS))
-    copies += [(part, around.at[pl.ds(i * ROWS, ROWS), :]) for i, part in enumerate(parts)]
     copies = [pltpu.make_async_copy(source, target, sems.at[i]) for i, (source, target) in enumerate(copies)]
     for copy in copies:
         copy.start()
@@ -267,13 +265,16 @@
     table = table + swapped(table, lambda z: z ^ 2)
     third = swapped(table, lambda z: z ^ 1)
 
+    blocks = [jnp.maximum(pole - 1, 0), pole, jnp.minimum(pole + 1, n_pole - 1)]
+    around = jnp.concatenate([lax.dynamic_slice_in_dim(depth, b * ROWS, ROWS, 0) for b in blocks])
+
     column = shape(6 * ROWS, LANES)
-    to_right, to_left, around = pl.pallas_call(
+    to_right, to_left = pl.pallas_call(
         edges_kernel,
-        out_shape=[column, column, shape(3 * ROWS, COLS)],
+        out_shape=[column, column],
         in_specs=[pl.BlockSpec(memory_space=pl.ANY)] * 4,
-        out_specs=[VMEM] * 3,
-        scratch_shapes=[pltpu.SemaphoreType.DMA((15,))],
+        out_specs=[VMEM] * 2,
+        scratch_shapes=[pltpu.SemaphoreType.DMA((12,))],
         compiler_params=pltpu.CompilerParams(vmem_limit_bytes=66600000),
     )(height, east_wind, north_wind, depth)
     from_left = lax.ppermute(to_right, "lon", [(i, (i + 1) % n_lon) for i in range(n_lon)])

time: 35.2 us -> 35.2 us (level)
  the two profiles are of different devices: /device:TPU:8 before, /device:TPU:32 now
where the time goes in v5:
time: 35.2 us; the launch traced here: 34.9 us
  starting transfers between devices  15.8 us (45%)
  waiting for transfers between devices  8.35 us (24%)
  Pallas kernels  7.21 us (20%)
  between operations  2.65 us (8%)
  local copies, waits for them, and re-layouts  0.81 us (2%)
    ppermute x3, starting transfers between devices, swapped(): return lax.ppermute(table, 'pole', pairs)  6.66 us
    pallas_call x1, Pallas kernels, body(): call(solve_kernel, [shape(ROWS, COLS)], 9, 60000000, scratch)  5.56 us
    ppermute x1, starting transfers between devices, body(): far = lax.ppermute(send_far, ('pole', 'lat', 'lon'), far_pairs)  4.32 us
    ppermute x1, waiting for transfers between devices, body(): near = lax.ppermute(send_near, 'pole', [(i, i ^ 1) for i in range(n_pole)])  3.92 us
    ppermute x3, waiting for transfers between devices, swapped(): return lax.ppermute(table, 'pole', pairs)  3.53 us
    ppermute x1, starting transfers between devices, body(): lax.ppermute(to_left, 'lon', [((i + 1) % n_lon, i) for i in range(n_lon)])  1.66 us
    ppermute x1, starting transfers between devices, body(): lax.ppermute(to_right, 'lon', [(i, (i + 1) % n_lon) for i in range(n_lon)])  1.65 us
    pallas_call x1, Pallas kernels, body(): pl.pallas_call(edges_kernel, out_shape=[column, column], in_specs=[pl.Blo...  1.54 us
  transfers between devices with their start and end apart: 7, of which 4 were waited for; matrix products, arithmetic and copies ran while one was open for 2% of the time, Pallas kernels for 5%

profile of v5, /device:TPU:32, one launch (start us, length us, event | category | flops | bytes accessed | tf_op | source)
XLA Modules:
  0.0 34.9 jit_solution(7585309769770646014)
XLA Ops:
  2.6 5.9 %collective-permute-start.2 = (f32[1,128]{1,0:T(1,128)S(1)}, f32[1,128]{1,0:T(1,128)S(1)}, u32[]{:S(2)}, u32[]{:S(2)}) collective-permute-start(f32[1,128]{1,0:T(1,128)S(1)} %compare_select_fusion.3), channel_id=1, source_target_pairs={{0,224},{16,240},{32,192},{48,208},{64,160},{80,176},{96,128},{112... | collective-permute-start | bytes 1544 | tf_op jit(solution)/shard_map/ppermute | solution.py:262
  8.5 1.5 %shard_map.82 = (f32[48,128]{1,0:T(8,128)}, f32[48,128]{1,0:T(8,128)}) custom-call(f32[8,1024]{1,0:T(8,128)} %height.3, f32[8,1024]{1,0:T(8,128)} %east.3, f32[8,1024]{1,0:T(8,128)} %north.3, f32[128,1024]{1,0:T(8,128)} %depth.1), custom_call_target="tpu_custom_call" | custom-call | tf_op jit(solution)/shard_map/pallas_call | solution.py:272
  10.1 1.7 %collective-permute-start = (f32[48,128]{1,0:T(8,128)}, f32[48,128]{1,0:T(8,128)S(1)}, u32[]{:S(2)}, u32[]{:S(2)}) collective-permute-start(f32[48,128]{1,0:T(8,128)} %get-tuple-element.14), channel_id=1, source_target_pairs={{0,1},{1,2},{2,3},{3,0},{4,5},{5,6},{6,7},{7,4},{8,9},{9,10},{10,1... | collective-permute-start | bytes 73736 | tf_op jit(solution)/shard_map/ppermute | solution.py:280
  11.7 1.7 %collective-permute-start.1 = (f32[48,128]{1,0:T(8,128)}, f32[48,128]{1,0:T(8,128)S(1)}, u32[]{:S(2)}, u32[]{:S(2)}) collective-permute-start(f32[48,128]{1,0:T(8,128)} %get-tuple-element.15), channel_id=1, source_target_pairs={{1,0},{2,1},{3,2},{0,3},{5,4},{6,5},{7,6},{4,7},{9,8},{10,9},{11,1... | collective-permute-start | bytes 73736 | tf_op jit(solution)/shard_map/ppermute | solution.py:281
  13.4 0.8 %constant_dynamic-slice_fusion.2 = (f32[8,1024]{1,0:T(8,128)S(1)}, f32[8,1024]{1,0:T(8,128)S(1)}, f32[8,1024]{1,0:T(8,128)S(1)}) fusion(f32[128,1024]{1,0:T(8,128)} %depth.1, s32[]{:T(128)S(6)} %select_n.54, s32[]{:T(128)S(6)} %select_n.55, s32[]{:T(128)S(6)} %select_n.56), kind=kLoop, calls=%fused_computation.7 | loop fusion | bytes 196620 | tf_op jit(solution)/shard_map/dynamic_slice | solution.py:269
  14.2 0.0 collective-permute-done.2
  14.2 0.6 %collective-permute-start.3 = (f32[1,128]{1,0:T(1,128)S(1)}, f32[1,128]{1,0:T(1,128)S(1)}, u32[]{:S(2)}, u32[]{:S(2)}) collective-permute-start(f32[1,128]{1,0:T(1,128)S(1)} %fusion.after), channel_id=1, source_target_pairs={{0,64},{16,80},{32,96},{48,112},{64,0},{80,16},{96,32},{112,48},{1... | collective-permute-start | bytes 1544 | tf_op jit(solution)/shard_map/ppermute | solution.py:262
  14.9 0.0 copy-start
  14.9 0.0 copy-start.1
  14.9 0.0 copy-start.2
  14.9 0.5 %collective-permute-done.from_left = f32[48,128]{1,0:T(8,128)S(1)} collective-permute-done((f32[48,128]{1,0:T(8,128)}, f32[48,128]{1,0:T(8,128)S(1)}, u32[]{:S(2)}, u32[]{:S(2)}) %collective-permute-start) | collective-permute-done | bytes 24608 | tf_op jit(solution)/shard_map/ppermute | solution.py:280
  15.4 0.4 %collective-permute-done.1.from_right = f32[48,128]{1,0:T(8,128)S(1)} collective-permute-done((f32[48,128]{1,0:T(8,128)}, f32[48,128]{1,0:T(8,128)S(1)}, u32[]{:S(2)}, u32[]{:S(2)}) %collective-permute-start.1) | collective-permute-done | bytes 24608 | tf_op jit(solution)/shard_map/ppermute | solution.py:281
  15.8 0.0 copy-done
  15.8 0.0 copy-done.1
  15.8 0.0 copy-done.2
  15.8 0.1 shard_map.83
  15.9 4.3 %collective-permute-start.6 = (f32[16,1152]{1,0:T(8,128)S(1)}, f32[16,1152]{1,0:T(8,128)S(1)}, u32[]{:S(2)}, u32[]{:S(2)}) collective-permute-start(f32[16,1152]{1,0:T(8,128)S(1)} %get-tuple-element.20), channel_id=1, source_target_pairs={{16,32},{32,16},{17,33},{33,17},{18,34},{34,18},{19,35},{35,19},{4... | collective-permute-start | bytes 221192 | tf_op jit(solution)/shard_map/ppermute | solution.py:294
  20.2 0.0 collective-permute-done.3
  20.2 0.1 collective-permute-start.4
  20.3 3.5 %collective-permute-done.4.two = f32[1,128]{1,0:T(1,128)S(1)} collective-permute-done((f32[1,128]{1,0:T(1,128)S(1)}, f32[1,128]{1,0:T(1,128)S(1)}, u32[]{:S(2)}, u32[]{:S(2)}) %collective-permute-start.4) | collective-permute-done | bytes 544 | tf_op jit(solution)/shard_map/ppermute | solution.py:262
  23.9 1.5 %collective-permute-start.5 = (f32[8,1152]{1,0:T(8,128)S(1)}, f32[8,1152]{1,0:T(8,128)S(1)}, u32[]{:S(2)}, u32[]{:S(2)}) collective-permute-start(f32[8,1152]{1,0:T(8,128)S(1)} %shard_map.84), channel_id=1, source_target_pairs={{0,16},{16,0},{32,48},{48,32},{64,80},{80,64},{96,112},{112,96},{1... | collective-permute-start | bytes 110600 | tf_op jit(solution)/shard_map/ppermute | solution.py:302
  25.4 3.9 %collective-permute-done.5.near = f32[8,1152]{1,0:T(8,128)S(1)} collective-permute-done((f32[8,1152]{1,0:T(8,128)S(1)}, f32[8,1152]{1,0:T(8,128)S(1)}, u32[]{:S(2)}, u32[]{:S(2)}) %collective-permute-start.5) | collective-permute-done | bytes 36896 | tf_op jit(solution)/shard_map/ppermute | solution.py:302
  29.3 0.0 collective-permute-done.6.far
  29.3 5.6 %shard_map.85 = f32[8,1024]{1,0:T(8,128)} custom-call(f32[8,1152]{1,0:T(8,128)S(1)} %get-tuple-element.16.field, f32[8,1152]{1,0:T(8,128)S(1)} %get-tuple-element.17.winds, f32[24,1152]{1,0:T(8,128)S(1)} %get-tuple-element.18.depths, f32[8,1152]{1,0:T(8,128)S(1)} %collective-permute-done.5.near, f32[16,1152]{1,0:T(8,128)S(1)} %collective-permute-done.6.far, ...), custom_call_target="tpu_custom_call" | custom-call | flops 60000000 | bytes 200000 | tf_op jit(solution)/shard_map/pallas_call | solution.py:317
  (5 shorter events, 0.0 us)
Async XLA Ops:
  2.6 11.6 %collective-permute-start.2 = (f32[1,128]{1,0:T(1,128)S(1)}, f32[1,128]{1,0:T(1,128)S(1)}, u32[]{:S(2)}, u32[]{:S(2)}) collective-permute-start(f32[1,128]{1,0:T(1,128)S(1)} %compare_select_fusion.3), channel_id=1, source_target_pairs={{0,224},{16,240},{32,192},{48,208},{64,160},{80,176},{96,128},{112... | collective-permute-start | bytes 1544 | tf_op jit(solution)/shard_map/ppermute | solution.py:262
  10.1 5.3 %collective-permute-start = (f32[48,128]{1,0:T(8,128)}, f32[48,128]{1,0:T(8,128)S(1)}, u32[]{:S(2)}, u32[]{:S(2)}) collective-permute-start(f32[48,128]{1,0:T(8,128)} %get-tuple-element.14), channel_id=1, source_target_pairs={{0,1},{1,2},{2,3},{3,0},{4,5},{5,6},{6,7},{7,4},{8,9},{9,10},{10,1... | collective-permute-start | bytes 73736 | tf_op jit(solution)/shard_map/ppermute | solution.py:280
  11.7 4.0 %collective-permute-start.1 = (f32[48,128]{1,0:T(8,128)}, f32[48,128]{1,0:T(8,128)S(1)}, u32[]{:S(2)}, u32[]{:S(2)}) collective-permute-start(f32[48,128]{1,0:T(8,128)} %get-tuple-element.15), channel_id=1, source_target_pairs={{1,0},{2,1},{3,2},{0,3},{5,4},{6,5},{7,6},{4,7},{9,8},{10,9},{11,1... | collective-permute-start | bytes 73736 | tf_op jit(solution)/shard_map/ppermute | solution.py:281
  14.2 6.0 %collective-permute-start.3 = (f32[1,128]{1,0:T(1,128)S(1)}, f32[1,128]{1,0:T(1,128)S(1)}, u32[]{:S(2)}, u32[]{:S(2)}) collective-permute-start(f32[1,128]{1,0:T(1,128)S(1)} %fusion.after), channel_id=1, source_target_pairs={{0,64},{16,80},{32,96},{48,112},{64,0},{80,16},{96,32},{112,48},{1... | collective-permute-start | bytes 1544 | tf_op jit(solution)/shard_map/ppermute | solution.py:262
  14.9 0.9 %copy-start = (f32[8,1024]{1,0:T(8,128)S(1)}, f32[8,1024]{1,0:T(8,128)}, u32[]{:S(2)}) copy-start(f32[8,1024]{1,0:T(8,128)} %height.3) | copy-start | bytes 98308
  14.9 0.9 %copy-start.1 = (f32[8,1024]{1,0:T(8,128)S(1)}, f32[8,1024]{1,0:T(8,128)}, u32[]{:S(2)}) copy-start(f32[8,1024]{1,0:T(8,128)} %east.3) | copy-start | bytes 98308
  14.9 0.9 %copy-start.2 = (f32[8,1024]{1,0:T(8,128)S(1)}, f32[8,1024]{1,0:T(8,128)}, u32[]{:S(2)}) copy-start(f32[8,1024]{1,0:T(8,128)} %north.3) | copy-start | bytes 98308
  15.9 13.4 %collective-permute-start.6 = (f32[16,1152]{1,0:T(8,128)S(1)}, f32[16,1152]{1,0:T(8,128)S(1)}, u32[]{:S(2)}, u32[]{:S(2)}) collective-permute-start(f32[16,1152]{1,0:T(8,128)S(1)} %get-tuple-element.20), channel_id=1, source_target_pairs={{16,32},{32,16},{17,33},{33,17},{18,34},{34,18},{19,35},{35,19},{4... | collective-permute-start | bytes 221192 | tf_op jit(solution)/shard_map/ppermute | solution.py:294
  20.2 3.6 %collective-permute-start.4 = (f32[1,128]{1,0:T(1,128)S(1)}, f32[1,128]{1,0:T(1,128)S(1)}, u32[]{:S(2)}, u32[]{:S(2)}) collective-permute-start(f32[1,128]{1,0:T(1,128)S(1)} %fusion.1.one), channel_id=1, source_target_pairs={{0,32},{16,48},{32,0},{48,16},{64,96},{80,112},{96,64},{112,80},{1... | collective-permute-start | bytes 1544 | tf_op jit(solution)/shard_map/ppermute | solution.py:262
  23.9 5.5 %collective-permute-start.5 = (f32[8,1152]{1,0:T(8,128)S(1)}, f32[8,1152]{1,0:T(8,128)S(1)}, u32[]{:S(2)}, u32[]{:S(2)}) collective-permute-start(f32[8,1152]{1,0:T(8,128)S(1)} %shard_map.84), channel_id=1, source_target_pairs={{0,16},{16,0},{32,48},{48,32},{64,80},{80,64},{96,112},{112,96},{1... | collective-permute-start | bytes 110600 | tf_op jit(solution)/shard_map/ppermute | solution.py:302
